TPU v7x, 32 devices: a whole 2x2x4 slice. The times are simulated.
32 devices in a mesh: pipe: 4 (over x, core), dp: 4 (over z), tensor: 2 (over y).
Axes of the slice: x: 2, y: 2, z: 4, core: 2. Of those that a mesh axis runs over, the one named last changes fastest.
Arguments:
- hidden_states: bfloat16 [4, 1024, 8192], P('pipe', 'dp'), may hold values from -60 to 60
- norm_gain: bfloat16 [4, 8192], P('pipe'), may hold values from 0.5 to 2
- key_weight: bfloat16 [4, 8192, 512], P('pipe', 'dp', 'tensor'), may hold values from -0.0625 to 0.0625
- value_weight: bfloat16 [4, 8192, 512], P('pipe', 'dp', 'tensor'), may hold values from -0.0625 to 0.0625
- queries: bfloat16 [4, 1024, 4096], P('pipe', 'dp', 'tensor'), may hold values from -128 to 128
- context_cotangent: bfloat16 [4, 1024, 4096], P('pipe', 'dp', 'tensor'), may hold values from -96 to 96
- lengths: int32 [4, 4], P('pipe', 'dp'), may hold values from 64 to 256, as said below
- policy_logp: float32 [4, 4], P('pipe', 'dp'), may hold values from -90 to -30
- reference_logp: float32 [4, 4], P('pipe', 'dp'), may hold values from -90 to -30
Outputs:
- key_weight_grad: bfloat16 [4, 8192, 512], P('pipe', 'dp', 'tensor')
- value_weight_grad: bfloat16 [4, 8192, 512], P('pipe', 'dp', 'tensor')
- lower_cotangent: bfloat16 [4, 1024, 8192], P('pipe', 'dp')
Inputs may be any that keep to these rules, and one draw needn't show every extreme that they name: `lengths`: each sequence's live tokens; positions at or beyond it are padding.
All inputs are finite; a program needn't handle non-finite values.
Results may differ from a plain program's by a relative error of at most 0.015.
The roundings to bfloat16 on the way count: a program that leaves them out, or rounds other values in their place, can miss the bound.
Values may be sent and summed in bfloat16 or wider, within the bound.
A program may use at most 128 MiB of HBM per device.

v0:
```python
import math

import jax
import jax.numpy as jnp
from jax import lax
from jax.sharding import PartitionSpec as P

HD = 128


npo_beta = 0.1
norm_eps = 1e-05
rope_base = 500000.0


def shifted(value, axis, steps):
    count = lax.axis_size(axis)
    leading, last = (max(0, -steps), min(count, count - steps))
    return lax.ppermute(value, axis, [(source, source + steps) for source in range(leading, last)])


def rope_tables(length, head_dim):
    positions = jnp.arange(length).astype(jnp.float32)
    freq_index = jnp.arange(head_dim // 2).astype(jnp.float32)
    inverse = 1.0 / rope_base ** (2.0 * freq_index / head_dim)
    angles = positions[:, None] * inverse[None, :]
    cosine = jnp.concatenate([jnp.cos(angles), jnp.cos(angles)], axis=1)
    sine = jnp.concatenate([jnp.sin(angles), jnp.sin(angles)], axis=1)
    return (cosine, sine)


def rotate_half(values):
    half = values.shape[-1] // 2
    return jnp.concatenate([-values[..., half:], values[..., :half]], axis=-1)


def rotate_back(values):
    half = values.shape[-1] // 2
    return jnp.concatenate([values[..., half:], -values[..., :half]], axis=-1)


def sequence_grads(query_seq, key_seq, value_seq, cotan_seq, length_seq, cosine, sine):
    seq_len, kv_heads, head_dim = key_seq.shape
    group = query_seq.shape[1] // kv_heads
    scale = 1.0 / math.sqrt(head_dim)
    query_g = query_seq.reshape(seq_len, kv_heads, group, head_dim)
    cotan_g = cotan_seq.reshape(seq_len, kv_heads, group, head_dim)
    scores = (
        jnp.einsum("ikgd,jkd->kgij", query_g, key_seq, preferred_element_type=jnp.float32) * scale
    )
    row_pos = jnp.arange(seq_len)[:, None]
    col_pos = jnp.arange(seq_len)[None, :]
    allowed = (col_pos <= row_pos) & (col_pos < length_seq)
    scores = jnp.where(allowed, scores, -1e30)
    highest = jnp.max(scores, axis=-1, keepdims=True)
    expd = jnp.where(allowed, jnp.exp(scores - highest), 0.0)
    probs = expd / jnp.sum(expd, axis=-1, keepdims=True)
    probs_low = probs.astype(jnp.bfloat16)
    value_grad = jnp.einsum(
        "kgij,ikgd->jkd", probs_low, cotan_g, preferred_element_type=jnp.float32
    ).astype(jnp.bfloat16)
    prob_grad = jnp.einsum("ikgd,jkd->kgij", cotan_g, value_seq, preferred_element_type=jnp.float32)
    centre = jnp.sum(probs * prob_grad, axis=-1, keepdims=True)
    score_grad = (probs * (prob_grad - centre) * scale).astype(jnp.bfloat16)
    rotated_grad = jnp.einsum(
        "kgij,ikgd->jkd", score_grad, query_g, preferred_element_type=jnp.float32
    )
    key_grad = rotated_grad * cosine[:, None, :] + rotate_back(rotated_grad * sine[:, None, :])
    return (key_grad.astype(jnp.bfloat16), value_grad)


def norm_backward(normed_grad, gain_f, nhat, inv_rms):
    gain_grad_in = normed_grad * gain_f
    centre = jnp.mean(gain_grad_in * nhat, axis=-1, keepdims=True)
    return ((gain_grad_in - nhat * centre) * inv_rms).astype(jnp.bfloat16)


def on_device(
    hidden_states,
    norm_gain,
    key_weight,
    value_weight,
    queries,
    context_cotangent,
    lengths,
    policy_logp,
    reference_logp,
):
    key_full, value_full = (
        lax.all_gather(key_weight[0], "dp", axis=0, tiled=True),
        lax.all_gather(value_weight[0], "dp", axis=0, tiled=True),
    )
    hidden = hidden_states[0]
    gain_f = norm_gain[0].astype(jnp.float32)
    tok_rows = hidden.shape[0]
    width_all = hidden.shape[1]
    seq_count = lengths.shape[1]
    seq_len = tok_rows // seq_count
    kv_cols = key_full.shape[1]
    kv_local = kv_cols // HD
    q_local = queries.shape[2] // HD
    hidden_f = hidden.astype(jnp.float32)
    inv_rms = lax.rsqrt(jnp.mean(hidden_f * hidden_f, axis=-1, keepdims=True) + norm_eps)
    nhat = hidden_f * inv_rms
    normed = (nhat * gain_f).astype(jnp.bfloat16)
    key_raw = jnp.dot(normed, key_full, preferred_element_type=jnp.float32)
    values = jnp.dot(normed, value_full, preferred_element_type=jnp.float32).astype(jnp.bfloat16)
    cosine, sine = rope_tables(seq_len, HD)
    key_four = key_raw.reshape(seq_count, seq_len, kv_local, HD)
    keys = (
        key_four * cosine[None, :, None, :] + rotate_half(key_four) * sine[None, :, None, :]
    ).astype(jnp.bfloat16)
    total_seqs = seq_count * lax.axis_size("dp")
    seq_weight = 2.0 * jax.nn.sigmoid(npo_beta * (policy_logp[0] - reference_logp[0])) / total_seqs
    live = jnp.arange(seq_len)[None, :] < lengths[0][:, None]
    factor = jnp.where(live, seq_weight[:, None], 0.0)
    scaled = (
        context_cotangent[0].reshape(seq_count, seq_len, q_local, HD).astype(jnp.float32)
        * factor[:, :, None, None]
    ).astype(jnp.bfloat16)

    def one_sequence(items):
        return sequence_grads(items[0], items[1], items[2], items[3], items[4], cosine, sine)

    key_grad, value_grad = lax.map(
        one_sequence,
        (
            queries[0].reshape(seq_count, seq_len, q_local, HD),
            keys,
            values.reshape(seq_count, seq_len, kv_local, HD),
            scaled,
            lengths[0],
        ),
    )
    key_grad = key_grad.reshape(tok_rows, kv_cols)
    value_grad = value_grad.reshape(tok_rows, kv_cols)
    combined = jnp.concatenate([key_grad, value_grad], axis=1)
    own_rows = width_all // lax.axis_size("dp")
    columns = lax.all_to_all(normed, "dp", split_axis=1, concat_axis=0, tiled=True)
    piece = lax.all_gather(combined, "dp", axis=0, tiled=True)
    count = piece.shape[0]
    sources = count // tok_rows
    block = columns.reshape(sources, tok_rows, own_rows)
    terms = jnp.einsum(
        "src,srd->scd",
        block,
        piece.reshape(sources, tok_rows, 2 * kv_cols),
        preferred_element_type=jnp.float32,
    )
    rounded = lax.optimization_barrier(terms.astype(jnp.bfloat16))
    grad_total = jnp.sum(rounded.astype(jnp.float32), axis=0)
    grad_low = grad_total.astype(jnp.bfloat16)
    part = lax.dot_general(
        key_grad, key_full, (((1,), (1,)), ((), ())), preferred_element_type=jnp.float32
    )
    part = part + lax.dot_general(
        value_grad, value_full, (((1,), (1,)), ((), ())), preferred_element_type=jnp.float32
    )
    normed_grad = lax.psum(part.astype(jnp.bfloat16), "tensor").astype(jnp.float32)
    section_cot = norm_backward(normed_grad, gain_f, nhat, inv_rms)
    lower = shifted(section_cot, "pipe", -1)
    return (grad_low[:, :kv_cols][None], grad_low[:, kv_cols:][None], lower[None])


def solution(mesh):
    in_specs = (
        P("pipe", "dp", None),
        P("pipe", None),
        P("pipe", "dp", "tensor"),
        P("pipe", "dp", "tensor"),
        P("pipe", "dp", "tensor"),
        P("pipe", "dp", "tensor"),
        P("pipe", "dp"),
        P("pipe", "dp"),
        P("pipe", "dp"),
    )
    out_specs = (P("pipe", "dp", "tensor"), P("pipe", "dp", "tensor"), P("pipe", "dp", None))
    return jax.shard_map(
        on_device, mesh=mesh, in_specs=in_specs, out_specs=out_specs, check_vma=False
    )
```

profile of v0, /device:TPU:0, one launch (start us, length us, event | category | flops | bytes accessed | tf_op | source)
XLA Modules:
  0.0 384.9 jit_solution(13934739434867706725)
XLA Ops:
  7.2 0.0 copy-start.3
  7.2 0.0 all-gather.8.cloned.1.call-start
  7.2 0.7 all-gather.8.cloned.1.call-update
  7.9 0.0 all-gather.10.cloned.1.call-start
  8.0 0.7 all-gather.10.cloned.1.call-update
  8.7 0.0 all-reduce.2.cloned.1.call-start
  10.7 0.8 convert_element_type.109
  11.5 0.0 copy-start.5
  11.6 0.3 multiply_cosine_fusion
  11.9 0.8 copy.13
  12.7 0.8 copy.17
  13.4 2.3 copy.38
  15.7 0.0 copy-done.3
  15.7 0.5 copy.35
  16.2 3.1 fusion.3
  19.3 0.7 fusion.39
  20.1 73.0 %all-gather.8.cloned.1.call-done = bf16[1,8192,256]{2,1,0:T(8,128)(2,1)} async-done(((bf16[1,2048,256]{2,1,0:T(8,128)(2,1)}), bf16[1,8192,256]{2,1,0:T(8,128)(2,1)}) %all-gather.8.cloned.1.call-update) | async-done | bytes 4194320 | tf_op jit(solution)/shard_map/all_gather | solution.py:90
  93.1 5.5 %fusion.12 = f32[256,256]{0,1:T(8,128)S(1)} fusion(bf16[1,8192,256]{2,1,0:T(8,128)(2,1)} %all-gather.8.cloned.1.call-done, bf16[1,256,8192]{2,1,0:T(8,128)(2,1)} %param.9, f32[8192]{0:T(1024)S(1)} %bitcast.126, f32[256]{0:T(256)S(1)} %add_rsqrt_fusion), kind=kOutput, calls=%fused_computation.24 | convolution fusion | flops 1082130432 | bytes 8684544 | tf_op jit(solution)/shard_map/dot_general | solution.py:106
  98.6 0.9 copy.14
  99.5 0.1 copy.36
  99.6 0.8 copy.37
  100.5 0.7 negate_bitcast_fusion
  101.2 72.8 %all-gather.10.cloned.1.call-done = bf16[1,8192,256]{2,1,0:T(8,128)(2,1)} async-done(((bf16[1,2048,256]{2,1,0:T(8,128)(2,1)}), bf16[1,8192,256]{2,1,0:T(8,128)(2,1)}) %all-gather.10.cloned.1.call-update) | async-done | bytes 4194320 | tf_op jit(solution)/shard_map/all_gather | solution.py:91
  174.0 0.0 copy-done.5
  174.0 5.6 %fusion.30 = bf16[256,256]{0,1:T(8,128)(2,1)S(1)} fusion(bf16[1,8192,256]{2,1,0:T(8,128)(2,1)} %all-gather.10.cloned.1.call-done, bf16[1,256,8192]{2,1,0:T(8,128)(2,1)} %param.9, f32[8192]{0:T(1024)S(1)} %bitcast.127, f32[256]{0:T(256)S(1)} %add_rsqrt_fusion), kind=kOutput, calls=%fused_computation.41 | convolution fusion | flops 1082195968 | bytes 8553472 | tf_op jit(solution)/shard_map/dot_general | solution.py:107
  179.6 0.0 copy-start.4
  179.6 0.0 copy-start.7
  179.6 2.7 fusion.33
  182.3 0.0 copy-done.4
  182.3 0.0 copy-done.7
  182.3 5.6 %fusion.47 = (f32[2,8,256]{2,1,0:T(8,128)}, f32[2,8,256,256]{2,3,1,0:T(8,128)}) fusion(pred[256,256]{0,1:T(8,128)(4,1)} %fusion.39, bf16[256,2,8,128]{0,3,2,1:T(8,128)(2,1)S(1)} %bitcast.120, f32[256,2,64]{2,0,1:T(8,128)} %bitcast.130, f32[256,2,64]{2,0,1:T(8,128)} %negate_bitcast_fusion, f32[256,2,128]{2,0,1:T(8,128)} %copy.14, f32[256,128]{1,0:T(8,128)} %copy.17, ...), kind=kOutput, calls=%fused_computation.75 | convolution fusion | flops 274006272 | bytes 6111232 | tf_op jit(solution)/shard_map/while/body/eval_jaxpr/sub | solution.py:56
  188.0 3.0 fusion.27
  191.0 7.3 %fusion.23 = f32[2,256,128]{1,2,0:T(8,128)S(1)} fusion(bf16[256,2,8,128]{0,3,2,1:T(8,128)(2,1)S(1)} %bitcast.121, f32[2,256,256,8]{2,1,3,0:T(8,128)} %fusion.33, f32[2,8,256,256]{2,3,1,0:T(8,128)} %get-tuple-element.42, f32[2,8,256]{2,1,0:T(8,128)} %get-tuple-element.41), kind=kOutput, calls=%fused_computation.38 | convolution fusion | flops 275779840 | bytes 9715712 | tf_op jit(solution)/shard_map/while/body/eval_jaxpr/kgij,ikgd->jkd/dot_general | solution.py:65
  198.4 0.0 copy-start.2
  198.4 3.6 fusion.10
  202.1 0.0 copy-done.2
  202.1 3.6 fusion.2
  205.7 0.0 all-reduce.2.cloned.1.call-update
  205.7 0.0 copy-start.8
  205.7 7.2 %copy.12 = f32[1,256,8192]{1,2,0:T(8,128)} copy(bf16[1,256,8192]{2,1,0:T(8,128)(2,1)} %param.9) | data formatting | bytes 12582912 | tf_op jit(solution)/shard_map/convert_element_type | solution.py:102
  212.9 0.0 copy-done.8
  212.9 0.1 convert_reduce_fusion
  213.0 5.4 %multiply_convert_fusion.2 = bf16[256,4,2048]{0,2,1:T(8,128)(2,1)} fusion(f32[256,4,2048]{0,2,1:T(8,128)} %bitcast.114, f32[4,2048]{1,0:T(4,128)S(1)} %mul.180, f32[256]{0:T(256)S(1)} %add_rsqrt_fusion), kind=kLoop, calls=%fused_computation.11 | loop fusion | flops 6291456 | bytes 12616704 | tf_op jit(solution)/shard_map/convert_element_type | solution.py:105
  218.4 0.0 copy-start.6
  218.4 5.1 %all-to-all-start = ((bf16[256,4,2048]{0,2,1:T(8,128)(2,1)}), bf16[256,4,2048]{0,2,1:T(8,128)(2,1)}, u32[]{:S(2)}, u32[]{:S(2)}) async-start(bf16[256,4,2048]{0,2,1:T(8,128)(2,1)} %multiply_convert_fusion.2), calls=%async_computation | async-start | bytes 8388608 | tf_op jit(solution)/shard_map/all_to_all | solution.py:139
  223.4 0.0 all-gather.6.cloned.1.call-start
  223.5 88.7 %all-reduce.2.cloned.1.call-done = bf16[256,8192]{1,0:T(8,128)(2,1)} async-done(((bf16[256,8192]{1,0:T(8,128)(2,1)}), bf16[256,8192]{1,0:T(8,128)(2,1)}) %all-reduce.2.cloned.1.call-update) | async-done | bytes 4194320 | tf_op jit(solution)/shard_map/psum | solution.py:159
  312.2 0.0 copy-done.6
  312.2 0.0 copy-start
  312.2 5.4 %multiply_reduce_fusion = f32[256]{0:T(256)S(1)} fusion(bf16[256,8192]{1,0:T(8,128)(2,1)} %all-reduce.2.cloned.1.call-done, bf16[1,256,8192]{2,1,0:T(8,128)(2,1)} %param.9, f32[8192]{0:T(1024)S(1)} %bitcast.128, f32[256]{0:T(256)S(1)} %add_rsqrt_fusion), kind=kLoop, calls=%fused_computation.8 | loop fusion | flops 12582656 | bytes 8423424 | tf_op jit(solution)/shard_map/reduce_sum | solution.py:74
  317.6 0.0 copy-done
  317.6 0.5 copy-done.1
  318.2 3.6 multiply_convert_fusion
  321.7 1.3 collective-permute-start
  323.0 0.7 pad_maximum_fusion
  323.8 0.0 all-gather.6.cloned.1.call-update
  323.8 33.1 %all-gather.6.cloned.1.call-done = bf16[1024,512]{0,1:T(8,128)(2,1)} async-done(((bf16[256,512]{0,1:T(8,128)(2,1)}), bf16[1024,512]{0,1:T(8,128)(2,1)}) %all-gather.6.cloned.1.call-update) | async-done | bytes 1048592 | tf_op jit(solution)/shard_map/all_gather | solution.py:140
  356.8 1.5 copy.25
  358.3 0.0 all-to-all-done
  358.3 7.8 %convolution_convert_fusion = bf16[4,2048,512]{2,1,0:T(8,128)(2,1)} fusion(bf16[4,256,512]{2,1,0:T(8,128)(2,1)S(1)} %bitcast.117, bf16[256,4,2048]{0,2,1:T(8,128)(2,1)} %all-to-all-done), kind=kOutput, calls=%fused_computation.12 | convolution fusion | flops 2151677952 | bytes 13631488 | tf_op jit(solution)/shard_map/src,srd->scd/dot_general | solution.py:144
  366.1 6.1 %reduce_sum.53 = bf16[2048,512]{1,0:T(8,128)(2,1)S(1)} reduce(bf16[4,2048,512]{2,1,0:T(8,128)(2,1)} %convolution_convert_fusion, bf16[]{:T(256)} %constant.53.clone.1), dimensions={0}, to_apply=%region_4.5 | reduce | flops 3145728 | bytes 10485762 | tf_op jit(solution)/shard_map/reduce_sum | solution.py:151
  372.2 1.5 slice_bitcast_fusion
  373.7 0.0 collective-permute-done
  373.7 4.6 %copy.44 = bf16[1,256,8192]{2,1,0:T(8,128)(2,1)} copy(bf16[1,256,8192]{2,1,0:T(8,128)(2,1)} %bitcast.32) | data formatting | bytes 8388608
  (13 shorter events, 0.2 us)
Async XLA Ops:
  7.2 8.5 %copy-start.3 = (bf16[1,256,2048]{2,1,0:T(8,128)(2,1)S(1)}, bf16[1,256,2048]{2,1,0:T(8,128)(2,1)}, u32[]{:S(2)}) copy-start(bf16[1,256,2048]{2,1,0:T(8,128)(2,1)} %param.14) | copy-start | bytes 3145732
  7.2 85.9 %all-gather.8.cloned.1.call-start = ((), (), s32[]{:S(2)}) async-start(), calls=%async_computation.3 | async-start | bytes 5242880 | tf_op jit(solution)/shard_map/all_gather | solution.py:90
  7.9 166.1 %all-gather.10.cloned.1.call-start = ((), (), s32[]{:S(2)}) async-start(), calls=%async_computation.4 | async-start | bytes 5242880 | tf_op jit(solution)/shard_map/all_gather | solution.py:91
  8.7 303.6 %all-reduce.2.cloned.1.call-start = ((), (), s32[]{:S(2)}) async-start(), calls=%async_computation.2 | async-start | bytes 8388608 | tf_op jit(solution)/shard_map/psum | solution.py:159
  11.5 162.4 %copy-start.5 = (f32[1,8192]{1,0:T(1,128)}, f32[1,8192]{1,0:T(1,128)S(1)}, u32[]{:S(2)}) copy-start(f32[1,8192]{1,0:T(1,128)S(1)} %convert_element_type.109) | copy-start | bytes 98308
  179.6 2.7 copy-start.4
  179.6 2.7 copy-start.7
  198.4 3.7 copy-start.2
  205.7 7.2 %copy-start.8 = (bf16[1,8192]{1,0:T(2,128)(2,1)S(1)}, bf16[1,8192]{1,0:T(2,128)(2,1)}, u32[]{:S(2)}) copy-start(bf16[1,8192]{1,0:T(2,128)(2,1)} %param.10) | copy-start | bytes 49156
  218.4 93.8 %copy-start.6 = (f32[1,8192]{1,0:T(1,128)S(1)}, f32[1,8192]{1,0:T(1,128)}, u32[]{:S(2)}) copy-start(f32[1,8192]{1,0:T(1,128)} %copy-done.5) | copy-start | bytes 98308
  218.4 139.9 %all-to-all-start = ((bf16[256,4,2048]{0,2,1:T(8,128)(2,1)}), bf16[256,4,2048]{0,2,1:T(8,128)(2,1)}, u32[]{:S(2)}, u32[]{:S(2)}) async-start(bf16[256,4,2048]{0,2,1:T(8,128)(2,1)} %multiply_convert_fusion.2), calls=%async_computation | async-start | bytes 8388608 | tf_op jit(solution)/shard_map/all_to_all | solution.py:139
  223.4 133.4 %all-gather.6.cloned.1.call-start = ((), (), s32[]{:S(2)}) async-start(), calls=%async_computation.1 | async-start | bytes 1310720 | tf_op jit(solution)/shard_map/all_gather | solution.py:140
  312.2 5.4 %copy-start = (bf16[1,256,8192]{2,1,0:T(8,128)(2,1)S(1)}, bf16[1,256,8192]{2,1,0:T(8,128)(2,1)}, u32[]{:S(2)}) copy-start(bf16[1,256,8192]{2,1,0:T(8,128)(2,1)} %param.9) | copy-start | bytes 12582916
  312.2 5.9 %copy-start.1 = (bf16[256,8192]{1,0:T(8,128)(2,1)S(1)}, bf16[256,8192]{1,0:T(8,128)(2,1)}, u32[]{:S(2)}) copy-start(bf16[256,8192]{1,0:T(8,128)(2,1)} %all-reduce.2.cloned.1.call-done) | copy-start | bytes 12582916
  321.7 52.0 %collective-permute-start = (bf16[256,8192]{1,0:T(8,128)(2,1)}, bf16[256,8192]{1,0:T(8,128)(2,1)}, u32[]{:S(2)}, u32[]{:S(2)}) collective-permute-start(bf16[256,8192]{1,0:T(8,128)(2,1)} %multiply_convert_fusion), channel_id=1, source_target_pairs={{8,0},{16,8},{24,16},{9,1},{17,9},{25,17},{10,2},{18,10},{26,18},{... | collective-permute-start | bytes 12582920 | tf_op jit(solution)/shard_map/ppermute | solution.py:19
Sparse Core Ops, SparseCore 0:
  9.6 83.4 all-gather.7
  94.6 79.2 all-gather.9
  205.8 106.3 all-reduce.1
  323.9 32.8 all-gather.5
where the time goes:
time: 386 us; the launch traced here: 385 us
  waiting for transfers between devices  269 us (70%)
  matrix products  44.8 us (12%)
  other arithmetic  27.1 us (7%)
  local copies, waits for them, and re-layouts  21.5 us (6%)
  between operations  16 us (4%)
  starting transfers between devices  6.49 us (2%)
    psum x1, waiting for transfers between devices, on_device(): lax.psum(part.astype(jnp.bfloat16), 'tensor').astype(jnp.float32)  88.7 us
    all_gather x1, waiting for transfers between devices, on_device(): lax.all_gather(key_weight[0], 'dp', axis=0, tiled=True)  73 us
    all_gather x1, waiting for transfers between devices, on_device(): lax.all_gather(value_weight[0], 'dp', axis=0, tiled=True)  72.8 us
    all_gather x1, waiting for transfers between devices, on_device(): piece = lax.all_gather(combined, 'dp', axis=0, tiled=True)  33.1 us
    dot_general x1, matrix products, on_device(): jnp.einsum('src,srd->scd', block, piece.reshape(sources, tok_rows, 2 * kv...  7.75 us
  transfers between devices with their start and end apart: 6, of which 4 were waited for; matrix products, arithmetic and copies ran while one was open for 15% of the time, Pallas kernels for 0%

commit v1 on v0

--- a/solution.py
+++ b/solution.py
@@ -1,8 +1,11 @@
+import functools
 import math
 
 import jax
 import jax.numpy as jnp
 from jax import lax
+from jax.experimental import pallas as pl
+from jax.experimental.pallas import tpu as pltpu
 from jax.sharding import PartitionSpec as P
 
 HD = 128
@@ -11,12 +14,6 @@
 npo_beta = 0.1
 norm_eps = 1e-05
 rope_base = 500000.0
-
-
-def shifted(value, axis, steps):
-    count = lax.axis_size(axis)
-    leading, last = (max(0, -steps), min(count, count - steps))
-    return lax.ppermute(value, axis, [(source, source + steps) for source in range(leading, last)])
 
 
 def rope_tables(length, head_dim):
@@ -69,10 +66,401 @@
     return (key_grad.astype(jnp.bfloat16), value_grad)
 
 
-def norm_backward(normed_grad, gain_f, nhat, inv_rms):
-    gain_grad_in = normed_grad * gain_f
-    centre = jnp.mean(gain_grad_in * nhat, axis=-1, keepdims=True)
-    return ((gain_grad_in - nhat * centre) * inv_rms).astype(jnp.bfloat16)
+MESH = pl.DeviceIdType.MESH
+VMEM_BYTES = 52 * 1024 * 1024
+
+
+def remote(src, dst, send_sem, recv_sem, **where):
+    return pltpu.make_async_remote_copy(
+        src_ref=src, dst_ref=dst, send_sem=send_sem, recv_sem=recv_sem,
+        device_id=where, device_id_type=MESH,
+    )
+
+
+def dot_nt(left, right):
+    return lax.dot_general(
+        left, right, (((1,), (1,)), ((), ())), preferred_element_type=jnp.float32
+    )
+
+
+def dot_tn(left, right):
+    return lax.dot_general(
+        left, right, (((0,), (0,)), ((), ())), preferred_element_type=jnp.float32
+    )
+
+
+FWD_CHUNKS = 2
+
+
+def project_kernel(
+    count, hid, gain, kw, vw,
+    cols_out, woth, inv_out, key_out, val_out,
+    normed, cols, total, psend, precv,
+    zs, zr, ws, wr, fs, fr, ps, pr, ls,
+):
+    z = lax.axis_index("dp")
+    y = lax.axis_index("tensor")
+    other = 1 - y
+    toks, width = hid.shape
+    rows = width // count
+    half_rows = rows // 2
+    half = toks // 2
+    chunk = half // FWD_CHUNKS
+    kcols = kw.shape[1]
+
+    barrier = pltpu.get_barrier_semaphore()
+    for d in range(1, count):
+        pl.semaphore_signal(
+            barrier, inc=1, device_id={"dp": lax.rem(z + d, count)}, device_id_type=MESH
+        )
+    pl.semaphore_signal(barrier, inc=1, device_id={"tensor": other}, device_id_type=MESH)
+    pl.semaphore_wait(barrier, count)
+
+    def norm_half(which):
+        def step(i, carry):
+            at = pl.ds(pl.multiple_of(which * half + i * 16, 16), 16)
+            h = hid[at, :].astype(jnp.float32)
+            inv = lax.rsqrt(jnp.mean(h * h, axis=-1, keepdims=True) + norm_eps)
+            normed[at, :] = (h * inv * gain[...]).astype(jnp.bfloat16)
+            inv_out[at, :] = jnp.broadcast_to(inv, (16, 128))
+            return carry
+
+        lax.fori_loop(0, half // 16, step, 0)
+
+    def rows_of(which, c):
+        return pl.ds(pl.multiple_of(which * half + c * chunk, 16), chunk)
+
+    norm_half(y)
+    sent = []
+    for c in range(FWD_CHUNKS):
+        for d in range(1, count):
+            to = lax.rem(z + d, count)
+            copy = remote(
+                normed.at[rows_of(y, c), pl.ds(pl.multiple_of(to * rows, 128), rows)],
+                cols.at[z, rows_of(y, c), :],
+                zs.at[c, d - 1], zr.at[c, d - 1], dp=to,
+            )
+            copy.start()
+            sent.append(copy)
+    give = pl.ds(pl.multiple_of(other * half_rows, 16), half_rows)
+    wcopies = [
+        remote(kw.at[give, :], woth.at[0], ws.at[0], wr.at[0], tensor=other),
+        remote(vw.at[give, :], woth.at[1], ws.at[1], wr.at[1], tensor=other),
+    ]
+    for copy in wcopies:
+        copy.start()
+    norm_half(other)
+    own = pltpu.make_async_copy(
+        normed.at[:, pl.ds(pl.multiple_of(z * rows, 128), rows)], cols.at[z], ls.at[count]
+    )
+    own.start()
+    own.wait()
+
+    step_k = min(rows, 512)
+
+    def project(src, c):
+        def step(k, acc):
+            at = pl.ds(pl.multiple_of(k * step_k, 128), step_k)
+            a = jnp.concatenate(
+                [cols[src, pl.ds(c * chunk, chunk), at], cols[src, pl.ds(half + c * chunk, chunk), at]],
+                axis=0,
+            )
+            return (
+                acc[0] + jnp.dot(a, kw[at, :], preferred_element_type=jnp.float32),
+                acc[1] + jnp.dot(a, vw[at, :], preferred_element_type=jnp.float32),
+            )
+
+        zero = jnp.zeros((2 * chunk, kcols), jnp.float32)
+        return lax.fori_loop(0, rows // step_k, step, (zero, zero))
+
+    for c in range(FWD_CHUNKS):
+        ka, va = project(z, c)
+        total[c, :, :kcols] = ka
+        total[c, :, kcols:] = va
+    outs = []
+    copy = pltpu.make_async_copy(cols.at[z], cols_out.at[z], ls.at[0])
+    copy.start()
+    outs.append(copy)
+
+    for c in range(FWD_CHUNKS):
+        for d in range(1, count):
+            src = lax.rem(z - d + count, count)
+            place = cols.at[src, rows_of(y, c), :]
+            remote(place, place, zs.at[c, d - 1], zr.at[c, d - 1], dp=src).wait_recv()
+            copy = remote(place, place, fs.at[c, d - 1], fr.at[c, d - 1], tensor=other)
+            copy.start()
+            sent.append(copy)
+        for d in range(1, count):
+            src = lax.rem(z - d + count, count)
+            place = cols.at[src, rows_of(other, c), :]
+            remote(place, place, fs.at[c, d - 1], fr.at[c, d - 1], tensor=other).wait_recv()
+            ka, va = project(src, c)
+            psend[d - 1, c, :, :kcols] = ka.astype(jnp.bfloat16)
+            psend[d - 1, c, :, kcols:] = va.astype(jnp.bfloat16)
+            copy = remote(
+                psend.at[d - 1, c], precv.at[d - 1, c], ps.at[c, d - 1], pr.at[c, d - 1], dp=src
+            )
+            copy.start()
+            sent.append(copy)
+            if c == FWD_CHUNKS - 1:
+                copy = pltpu.make_async_copy(cols.at[src], cols_out.at[src], ls.at[d])
+                copy.start()
+                outs.append(copy)
+    for c in range(FWD_CHUNKS):
+        acc = total[c]
+        for d in range(1, count):
+            remote(
+                psend.at[d - 1, c], precv.at[d - 1, c], ps.at[c, d - 1], pr.at[c, d - 1],
+                dp=lax.rem(z + d, count),
+            ).wait_recv()
+            acc = acc + precv[d - 1, c].astype(jnp.float32)
+        for which in range(2):
+            at = pl.ds(which * half + c * chunk, chunk)
+            part = acc[which * chunk : (which + 1) * chunk]
+            key_out[at, :] = part[:, :kcols]
+            val_out[at, :] = part[:, kcols:]
+    for copy in sent:
+        copy.wait_send()
+    for copy in wcopies:
+        copy.wait()
+    for copy in outs:
+        copy.wait()
+
+
+def project_call(hidden, gain_f, kw, vw, count):
+    toks, width = hidden.shape
+    rows = width // count
+    kcols = kw.shape[1]
+    vmem = pl.BlockSpec(memory_space=pltpu.VMEM)
+    hbm = pl.BlockSpec(memory_space=pl.ANY)
+    dma = pltpu.SemaphoreType.DMA
+    m = 2 * (toks // 2 // FWD_CHUNKS)
+    pair = (FWD_CHUNKS, count - 1)
+    return pl.pallas_call(
+        functools.partial(project_kernel, count),
+        out_shape=(
+            jax.ShapeDtypeStruct((count, toks, rows), jnp.bfloat16),
+            jax.ShapeDtypeStruct((2, rows // 2, kcols), jnp.bfloat16),
+            jax.ShapeDtypeStruct((toks, 128), jnp.float32),
+            jax.ShapeDtypeStruct((toks, kcols), jnp.float32),
+            jax.ShapeDtypeStruct((toks, kcols), jnp.float32),
+        ),
+        in_specs=[vmem] * 4,
+        out_specs=(hbm, hbm, vmem, vmem, vmem),
+        scratch_shapes=[
+            pltpu.VMEM((toks, width), jnp.bfloat16),
+            pltpu.VMEM((count, toks, rows), jnp.bfloat16),
+            pltpu.VMEM((FWD_CHUNKS, m, 2 * kcols), jnp.float32),
+            pltpu.VMEM((count - 1, FWD_CHUNKS, m, 2 * kcols), jnp.bfloat16),
+            pltpu.VMEM((count - 1, FWD_CHUNKS, m, 2 * kcols), jnp.bfloat16),
+            dma(pair), dma(pair), dma((2,)), dma((2,)), dma(pair), dma(pair), dma(pair), dma(pair),
+            dma((count + 1,)),
+        ],
+        compiler_params=pltpu.CompilerParams(
+            collective_id=0, has_side_effects=True, vmem_limit_bytes=VMEM_BYTES
+        ),
+        name="project",
+    )(hidden, gain_f, kw, vw)
+
+
+BWD_CHUNKS = 4
+
+
+def backward_kernel(
+    count, stages, comb, cpart, inv, hid, gain, kw, vw, woth, cols,
+    low, kg_out, vg_out,
+    pown, poth, ngs, ngr, cot, cother,
+    sa, ra, sb, rb, sc, rc, sn, rn, so, ro,
+):
+    p = lax.axis_index("pipe")
+    z = lax.axis_index("dp")
+    y = lax.axis_index("tensor")
+    other = 1 - y
+    toks, width = hid.shape
+    rows = width // count
+    half_rows = rows // 2
+    kcols = kw.shape[1]
+    chunk = toks // BWD_CHUNKS
+    has_lower = p > 0
+    has_upper = p < stages - 1
+
+    barrier = pltpu.get_barrier_semaphore()
+    for d in range(1, count):
+        pl.semaphore_signal(
+            barrier, inc=1, device_id={"dp": lax.rem(z + d, count)}, device_id_type=MESH
+        )
+    pl.semaphore_signal(barrier, inc=1, device_id={"tensor": other}, device_id_type=MESH)
+    for t in range(2):
+
+        @pl.when(has_lower)
+        def _():
+            pl.semaphore_signal(
+                barrier, inc=1, device_id={"pipe": p - 1, "tensor": t}, device_id_type=MESH
+            )
+
+        @pl.when(has_upper)
+        def _():
+            pl.semaphore_signal(
+                barrier, inc=1, device_id={"pipe": p + 1, "tensor": t}, device_id_type=MESH
+            )
+
+    peers = count + 2 * has_lower.astype(jnp.int32) + 2 * has_upper.astype(jnp.int32)
+    pl.semaphore_wait(barrier, peers)
+
+    sent = []
+    for d in range(1, count):
+        copy = remote(comb, pown.at[z], sa.at[d - 1], ra.at[d - 1], dp=lax.rem(z + d, count))
+        copy.start()
+        sent.append(copy)
+    copy = remote(comb, poth.at[z], sb.at[0], rb.at[0], tensor=other)
+    copy.start()
+    sent.append(copy)
+    ccopy = remote(cpart, cother, sc.at[0], rc.at[0], tensor=other)
+    ccopy.start()
+    pown[z] = comb[...]
+    for d in range(1, count):
+        src = lax.rem(z - d + count, count)
+        remote(comb, pown.at[src], sa.at[d - 1], ra.at[d - 1], dp=src).wait_recv()
+        copy = remote(pown.at[src], poth.at[src], sb.at[d], rb.at[d], tensor=other)
+        copy.start()
+        sent.append(copy)
+
+    tile = min(half_rows, 256)
+
+    def normed_grad(src, out, slot):
+        def step(n, carry):
+            mine = pl.ds(pl.multiple_of(y * half_rows + n * tile, 16), tile)
+            at = pl.ds(pl.multiple_of(n * tile, 128), tile)
+            a = dot_nt(pown[src, :, :kcols], kw[mine, :]) + dot_nt(pown[src, :, kcols:], vw[mine, :])
+            b = dot_nt(poth[src, :, :kcols], woth[0, at, :]) + dot_nt(poth[src, :, kcols:], woth[1, at, :])
+            both = a.astype(jnp.bfloat16).astype(jnp.float32) + b.astype(jnp.bfloat16).astype(jnp.float32)
+            out[slot, :, at] = both.astype(jnp.bfloat16)
+            return carry
+
+        lax.fori_loop(0, half_rows // tile, step, 0)
+
+    def wait_other(d):
+        src = lax.rem(z - d + count, count)
+        remote(pown.at[src], poth.at[src], sb.at[d], rb.at[d], tensor=other).wait_recv()
+
+    wait_other(0)
+    normed_grad(z, ngr, z)
+    for d in range(1, count):
+        wait_other(d)
+        normed_grad(lax.rem(z - d + count, count), ngs, d - 1)
+    for c in range(BWD_CHUNKS):
+        at = pl.ds(c * chunk, chunk)
+        for d in range(1, count):
+            copy = remote(
+                ngs.at[d - 1, at, :], ngr.at[z, at, :], sn.at[c, d - 1], rn.at[c, d - 1],
+                dp=lax.rem(z - d + count, count),
+            )
+            copy.start()
+            sent.append(copy)
+    ccopy.wait()
+
+    wtile = min(rows, 256)
+    wsteps = rows // wtile
+
+    def weight_grad(n, carry):
+        at = pl.ds(pl.multiple_of(n * wtile, 128), wtile)
+        acc = jnp.zeros((wtile, 2 * kcols), jnp.float32)
+        for r in range(count):
+            term = dot_tn(cols[r, :, at], pown[r])
+            acc = acc + term.astype(jnp.bfloat16).astype(jnp.float32)
+        low_acc = acc.astype(jnp.bfloat16)
+        kg_out[at, :] = low_acc[:, :kcols]
+        vg_out[at, :] = low_acc[:, kcols:]
+        return carry
+
+    def out_copy(c, w, k, up):
+        at = pl.ds(c * chunk, chunk)
+        half_at = y if (not up or k == 0) else other
+        feat = pl.ds(pl.multiple_of(w * rows + half_at * half_rows, 128), half_rows)
+        return remote(
+            cot.at[w, at, :], low.at[at, feat], so.at[c, w, k], ro.at[c, w, k],
+            pipe=p + 1 if up else p - 1, tensor=y if k == 0 else other,
+        )
+
+    for c in range(BWD_CHUNKS):
+        lax.fori_loop(wsteps * c // BWD_CHUNKS, wsteps * (c + 1) // BWD_CHUNKS, weight_grad, 0)
+        for d in range(1, count):
+            to = lax.rem(z + d, count)
+            remote(
+                ngs.at[d - 1, pl.ds(c * chunk, chunk), :], ngr.at[to, pl.ds(c * chunk, chunk), :],
+                sn.at[c, d - 1], rn.at[c, d - 1], dp=to,
+            ).wait_recv()
+
+        def tail(i, carry):
+            at = pl.ds(pl.multiple_of(c * chunk + i * 16, 16), 16)
+            inv_rms = inv[at, :][:, :1]
+            centre = (cpart[at, :] + cother[at, :])[:, :1] * (1.0 / width)
+            for w in range(count):
+                feat = pl.ds(pl.multiple_of(w * rows + y * half_rows, 128), half_rows)
+                nhat = hid[at, feat].astype(jnp.float32) * inv_rms
+                grad_in = ngr[w, at, :].astype(jnp.float32) * gain[:, feat]
+                cot[w, at, :] = ((grad_in - nhat * centre) * inv_rms).astype(jnp.bfloat16)
+            return carry
+
+        lax.fori_loop(0, chunk // 16, tail, 0)
+
+        @pl.when(has_lower)
+        def _():
+            for w in range(count):
+                for k in range(2):
+                    out_copy(c, w, k, False).start()
+
+    for copy in sent:
+        copy.wait_send()
+
+    @pl.when(has_lower)
+    def _():
+        for c in range(BWD_CHUNKS):
+            for w in range(count):
+                for k in range(2):
+                    out_copy(c, w, k, False).wait_send()
+
+    @pl.when(has_upper)
+    def _():
+        for c in range(BWD_CHUNKS):
+            for w in range(count):
+                for k in range(2):
+                    out_copy(c, w, k, True).wait_recv()
+
+
+def backward_call(comb, cpart, inv, hidden, gain_f, kw, vw, woth, cols, count, stages):
+    toks, width = hidden.shape
+    rows = width // count
+    kcols = kw.shape[1]
+    vmem = pl.BlockSpec(memory_space=pltpu.VMEM)
+    hbm = pl.BlockSpec(memory_space=pl.ANY)
+    dma = pltpu.SemaphoreType.DMA
+    pair = (BWD_CHUNKS, count - 1)
+    trio = (BWD_CHUNKS, count, 2)
+    return pl.pallas_call(
+        functools.partial(backward_kernel, count, stages),
+        out_shape=(
+            jax.ShapeDtypeStruct((toks, width), jnp.bfloat16),
+            jax.ShapeDtypeStruct((rows, kcols), jnp.bfloat16),
+            jax.ShapeDtypeStruct((rows, kcols), jnp.bfloat16),
+        ),
+        in_specs=[vmem] * 9,
+        out_specs=(hbm, vmem, vmem),
+        scratch_shapes=[
+            pltpu.VMEM((count, toks, 2 * kcols), jnp.bfloat16),
+            pltpu.VMEM((count, toks, 2 * kcols), jnp.bfloat16),
+            pltpu.VMEM((count - 1, toks, rows // 2), jnp.bfloat16),
+            pltpu.VMEM((count, toks, rows // 2), jnp.bfloat16),
+            pltpu.VMEM((count, toks, rows // 2), jnp.bfloat16),
+            pltpu.VMEM((toks, 128), jnp.float32),
+            dma((count - 1,)), dma((count - 1,)), dma((count,)), dma((count,)), dma((1,)), dma((1,)),
+            dma(pair), dma(pair), dma(trio), dma(trio),
+        ],
+        compiler_params=pltpu.CompilerParams(
+            collective_id=1, has_side_effects=True, vmem_limit_bytes=VMEM_BYTES
+        ),
+        name="backward",
+    )(comb, cpart, inv, hidden, gain_f, kw, vw, woth, cols)
 
 
 def on_device(
@@ -86,31 +474,25 @@
     policy_logp,
     reference_logp,
 ):
-    key_full, value_full = (
-        lax.all_gather(key_weight[0], "dp", axis=0, tiled=True),
-        lax.all_gather(value_weight[0], "dp", axis=0, tiled=True),
-    )
+    count = lax.axis_size("dp")
+    stages = lax.axis_size("pipe")
     hidden = hidden_states[0]
-    gain_f = norm_gain[0].astype(jnp.float32)
+    gain_f = norm_gain.astype(jnp.float32)
+    kw, vw = key_weight[0], value_weight[0]
     tok_rows = hidden.shape[0]
-    width_all = hidden.shape[1]
     seq_count = lengths.shape[1]
     seq_len = tok_rows // seq_count
-    kv_cols = key_full.shape[1]
+    kv_cols = kw.shape[1]
     kv_local = kv_cols // HD
     q_local = queries.shape[2] // HD
-    hidden_f = hidden.astype(jnp.float32)
-    inv_rms = lax.rsqrt(jnp.mean(hidden_f * hidden_f, axis=-1, keepdims=True) + norm_eps)
-    nhat = hidden_f * inv_rms
-    normed = (nhat * gain_f).astype(jnp.bfloat16)
-    key_raw = jnp.dot(normed, key_full, preferred_element_type=jnp.float32)
-    values = jnp.dot(normed, value_full, preferred_element_type=jnp.float32).astype(jnp.bfloat16)
+    cols, woth, inv, key_raw, val_raw = project_call(hidden, gain_f, kw, vw, count)
+    values = val_raw.astype(jnp.bfloat16)
     cosine, sine = rope_tables(seq_len, HD)
     key_four = key_raw.reshape(seq_count, seq_len, kv_local, HD)
     keys = (
         key_four * cosine[None, :, None, :] + rotate_half(key_four) * sine[None, :, None, :]
     ).astype(jnp.bfloat16)
-    total_seqs = seq_count * lax.axis_size("dp")
+    total_seqs = seq_count * count
     seq_weight = 2.0 * jax.nn.sigmoid(npo_beta * (policy_logp[0] - reference_logp[0])) / total_seqs
     live = jnp.arange(seq_len)[None, :] < lengths[0][:, None]
     factor = jnp.where(live, seq_weight[:, None], 0.0)
@@ -135,31 +517,16 @@
     key_grad = key_grad.reshape(tok_rows, kv_cols)
     value_grad = value_grad.reshape(tok_rows, kv_cols)
     combined = jnp.concatenate([key_grad, value_grad], axis=1)
-    own_rows = width_all // lax.axis_size("dp")
-    columns = lax.all_to_all(normed, "dp", split_axis=1, concat_axis=0, tiled=True)
-    piece = lax.all_gather(combined, "dp", axis=0, tiled=True)
-    count = piece.shape[0]
-    sources = count // tok_rows
-    block = columns.reshape(sources, tok_rows, own_rows)
-    terms = jnp.einsum(
-        "src,srd->scd",
-        block,
-        piece.reshape(sources, tok_rows, 2 * kv_cols),
-        preferred_element_type=jnp.float32,
-    )
-    rounded = lax.optimization_barrier(terms.astype(jnp.bfloat16))
-    grad_total = jnp.sum(rounded.astype(jnp.float32), axis=0)
-    grad_low = grad_total.astype(jnp.bfloat16)
-    part = lax.dot_general(
-        key_grad, key_full, (((1,), (1,)), ((), ())), preferred_element_type=jnp.float32
-    )
-    part = part + lax.dot_general(
-        value_grad, value_full, (((1,), (1,)), ((), ())), preferred_element_type=jnp.float32
-    )
-    normed_grad = lax.psum(part.astype(jnp.bfloat16), "tensor").astype(jnp.float32)
-    section_cot = norm_backward(normed_grad, gain_f, nhat, inv_rms)
-    lower = shifted(section_cot, "pipe", -1)
-    return (grad_low[:, :kv_cols][None], grad_low[:, kv_cols:][None], lower[None])
+    cpart = jnp.sum(
+        key_grad.astype(jnp.float32) * key_raw + value_grad.astype(jnp.float32) * val_raw,
+        axis=-1, keepdims=True,
+    )
+    cpart = jnp.broadcast_to(cpart, (tok_rows, 128))
+    low, kg, vg = backward_call(
+        combined, cpart, inv, hidden, gain_f, kw, vw, woth, cols, count, stages
+    )
+    low = jnp.where(lax.axis_index("pipe") < stages - 1, low, jnp.zeros_like(low))
+    return (kg[None], vg[None], low[None])
 
 
 def solution(mesh):

time: 386 us -> 226 us (0.59)
  waiting for transfers between devices: 269 us -> 0 us
  Pallas kernels: 0 us -> 189 us
  matrix products: 44.8 us -> 18 us
  other arithmetic: 27.1 us -> 6.81 us
  local copies, waits for them, and re-layouts: 21.5 us -> 6.57 us
  between operations: 16 us -> 2.86 us
  starting transfers between devices: 6.49 us -> 0 us
    pallas_call x0 -> x2, Pallas kernels: none -> 189 us  [the longest x1 107 us: backward_call(): pl.pallas_call(functools.partial(backward_kernel, count, stages), out_sha...]
    all_gather x3 -> x0, waiting for transfers between devices: 179 us -> none  [the longest x1 73 us: on_device(): lax.all_gather(key_weight[0], 'dp', axis=0, tiled=True)]
    psum x1 -> x0, waiting for transfers between devices: 88.7 us -> none  [on_device(): lax.psum(part.astype(jnp.bfloat16), 'tensor').astype(jnp.float32)]
    dot_general x5 -> x0, matrix products: 26.1 us -> none  [the longest x1 7.75 us: on_device(): jnp.einsum('src,srd->scd', block, piece.reshape(sources, tok_rows, 2 * kv...]
    reduce_sum x3 -> x1, other arithmetic: 14.6 us -> 0.13 us  [on_device(): jnp.sum(key_grad.astype(jnp.float32) * key_raw + value_grad.astype(jnp.fl...]
    convert_element_type x4 -> x2, other arithmetic: 9.88 us -> 0.81 us  [the longest x1 0.79 us: on_device(): gain_f = norm_gain.astype(jnp.float32)]
    convert_element_type x1 -> x0, local copies, waits for them, and re-layouts: 7.17 us -> none  [on_device(): hidden_f = hidden.astype(jnp.float32)]
    all_to_all x1 -> x0, starting transfers between devices: 5.05 us -> none  [on_device(): lax.all_to_all(normed, 'dp', split_axis=1, concat_axis=0, tiled=True)]
  transfers between devices with their start and end apart: 6 -> 0, of which waited for: 4 -> 0; matrix products, arithmetic and copies ran while one was open for 15% -> 0% of each run, Pallas kernels for 0% -> 0%
where the time goes in v1:
time: 226 us; the launch traced here: 224 us
  Pallas kernels  189 us (84%)
  matrix products  18 us (8%)
  other arithmetic  6.81 us (3%)
  local copies, waits for them, and re-layouts  6.57 us (3%)
  between operations  2.86 us (1%)
    pallas_call x1, Pallas kernels, backward_call(): pl.pallas_call(functools.partial(backward_kernel, count, stages), out_sha...  107 us
    pallas_call x1, Pallas kernels, project_call(): pl.pallas_call(functools.partial(project_kernel, count), out_shape=(jax.S...  82.4 us
    dot_general x1, matrix products, sequence_grads(): jnp.einsum('kgij,ikgd->jkd', score_grad, query_g, preferred_element_type=...  7.45 us
    sub x1, matrix products, sequence_grads(): expd = jnp.where(allowed, jnp.exp(scores - highest), 0.0)  4.86 us
    broadcast_in_dim x1, other arithmetic, on_device(): return (kg[None], vg[None], low[None])  4.57 us

profile of v1, /device:TPU:0, one launch (start us, length us, event | category | flops | bytes accessed | tf_op | source)
XLA Modules:
  0.0 223.5 jit_solution(887680717792679617)
XLA Ops:
  0.6 0.8 convert_element_type.78.gain
  1.4 0.0 copy-start.1
  1.4 82.4 %project.1 = (bf16[4,256,2048]{2,1,0:T(8,128)(2,1)}, bf16[2,1024,256]{2,1,0:T(8,128)(2,1)S(1)}, f32[256,128]{1,0:T(8,128)S(1)}, f32[256,256]{1,0:T(8,128)S(1)}, f32[256,256]{1,0:T(8,128)S(1)}) custom-call(bf16[256,8192]{1,0:T(8,128)(2,1)} %bitcast.94, f32[1,8192]{1,0:T(1,128)S(1)} %convert_element_type.78.gain, bf16[2048,256]{1,0:T(8,128)(2,1)} %bitcast.98, ...), custom_call_target="tpu_custom_call" | custom-call | tf_op jit(solution)/shard_map/project/pallas_call | solution.py:239
  83.9 0.0 copy-start
  83.9 1.0 copy-done
  84.9 0.1 reshape.105
  85.0 0.3 fusion.35
  85.3 0.7 copy_bitcast_fusion
  86.1 0.3 multiply_cosine_fusion
  86.4 0.1 copy.12
  86.5 0.8 copy.16
  87.3 0.0 copy-done.1
  87.3 0.5 copy.40
  87.8 0.0 copy-start.2
  88.5 0.1 fusion.27
  88.6 4.9 %fusion.36 = (f32[2,8,256]{2,1,0:T(8,128)S(1)}, f32[2,8,256,256]{2,3,1,0:T(8,128)}) fusion(pred[256,256]{0,1:T(8,128)(4,1)S(1)} %fusion.27, bf16[256,2,8,128]{0,3,2,1:T(8,128)(2,1)S(1)} %bitcast.102, f32[256,2,64]{2,0,1:T(8,128)S(1)} %get-tuple-element.57, f32[256,2,64]{2,0,1:T(8,128)} %get-tuple-element.58, f32[256,128]{1,0:T(8,128)} %copy.16, ...), kind=kOutput, calls=%fused_computation.56 | convolution fusion | flops 274006272 | bytes 6111232 | tf_op jit(solution)/shard_map/while/body/eval_jaxpr/sub | solution.py:53
  93.5 0.0 copy-done.2
  94.9 1.5 copy.35
  96.4 2.7 %fusion.20 = f32[2,256,256,8]{2,1,3,0:T(8,128)} fusion(f32[256,2,8,128]{0,3,2,1:T(8,128)S(1)} %bitcast.96, f32[256]{0:T(256)S(1)} %broadcast_select_fusion, bf16[256,2,128,1]{2,1,0,3:T(2,128)(2,1)S(1)} %bitcast.105), kind=kOutput, calls=%fused_computation.23 | convolution fusion | flops 269484032 | bytes 6423552 | tf_op jit(solution)/shard_map/while/body/eval_jaxpr/ikgd,jkd->kgij/dot_general | solution.py:59
  99.1 7.4 %fusion.13 = f32[2,256,128]{1,2,0:T(8,128)S(1)} fusion(bf16[256,2,8,128]{0,3,2,1:T(8,128)(2,1)} %bitcast.103, f32[2,256,256,8]{2,1,3,0:T(8,128)} %fusion.20, f32[2,8,256,256]{2,3,1,0:T(8,128)} %get-tuple-element.56, f32[2,8,256]{2,1,0:T(8,128)S(1)} %get-tuple-element.55), kind=kOutput, calls=%fused_computation.20 | convolution fusion | flops 275779840 | bytes 9715712 | tf_op jit(solution)/shard_map/while/body/eval_jaxpr/kgij,ikgd->jkd/dot_general | solution.py:62
  106.6 0.1 copy.36
  106.7 3.0 %fusion.17 = bf16[2,128,256]{2,1,0:T(8,128)(2,1)S(1)} fusion(f32[256,2,8,128]{0,3,2,1:T(8,128)S(1)} %bitcast.97, f32[256]{0:T(256)S(1)} %broadcast_select_fusion, f32[2,8,256,256]{2,3,1,0:T(8,128)} %get-tuple-element.56, f32[2,8,256]{2,1,0:T(8,128)S(1)} %get-tuple-element.55), kind=kOutput, calls=%fused_computation.22 | convolution fusion | flops 271646720 | bytes 6439936 | tf_op jit(solution)/shard_map/while/body/eval_jaxpr/kgij,ikgd->jkd/dot_general | solution.py:56
  109.8 0.1 copy.37
  109.9 0.1 add_reduce_fusion
  110.0 0.1 broadcast_in_dim.79.cpart
  110.1 106.8 %backward.1 = (bf16[256,8192]{1,0:T(8,128)(2,1)}, bf16[2048,256]{1,0:T(8,128)(2,1)S(1)}, bf16[2048,256]{1,0:T(8,128)(2,1)}) custom-call(bf16[256,512]{1,0:T(8,128)(2,1)S(1)} %pad_maximum_fusion.comb, f32[256,128]{1,0:T(8,128)S(1)} %broadcast_in_dim.79.cpart, f32[256,128]{1,0:T(8,128)S(1)} %get-tuple-element.43.inv, bf16[256,8192]{1,0:T(8,128)(2,1)} %bitcast.95, ...), custom_call_target="tpu_custom_call" | custom-call | tf_op jit(solution)/shard_map/backward/pallas_call | solution.py:440
  217.0 0.0 copy-start.3
  217.0 4.6 %select_bitcast_fusion = bf16[1,256,8192]{2,1,0:T(8,128)(2,1)} fusion(bf16[256,8192]{1,0:T(8,128)(2,1)} %get-tuple-element.48, pred[]{:T(512)S(6)} %lt.29), kind=kLoop, calls=%fused_computation.8 | loop fusion | flops 2097152 | bytes 8388609 | tf_op jit(solution)/shard_map/broadcast_in_dim | solution.py:529
  221.6 1.0 copy.59
  222.6 0.0 copy-done.3
  222.6 1.0 copy.60
  (11 shorter events, 0.2 us)
Async XLA Ops:
  1.4 85.9 %copy-start.1 = (bf16[1,256,2048]{2,1,0:T(8,128)(2,1)S(1)}, bf16[1,256,2048]{2,1,0:T(8,128)(2,1)}, u32[]{:S(2)}) copy-start(bf16[1,256,2048]{2,1,0:T(8,128)(2,1)} %param.13) | copy-start | bytes 3145732
  83.9 1.0 copy-start
  87.8 5.6 %copy-start.2 = (bf16[1,256,2048]{1,2,0:T(8,128)(2,1)}, bf16[1,256,2048]{1,2,0:T(8,128)(2,1)S(1)}, u32[]{:S(2)}) copy-start(bf16[1,256,2048]{1,2,0:T(8,128)(2,1)S(1)} %copy.40) | copy-start | bytes 3145732
  217.0 5.5 %copy-start.3 = (bf16[2048,256]{1,0:T(8,128)(2,1)S(1)}, bf16[2048,256]{1,0:T(8,128)(2,1)}, u32[]{:S(2)}) copy-start(bf16[2048,256]{1,0:T(8,128)(2,1)} %get-tuple-element.47) | copy-start | bytes 3145732

commit v2 on v1

v2 whole, which is shorter than its diff:
```python
import functools
import math

import jax
import jax.numpy as jnp
from jax import lax
from jax.experimental import pallas as pl
from jax.experimental.pallas import tpu as pltpu
from jax.sharding import PartitionSpec as P

HD = 128


npo_beta = 0.1
norm_eps = 1e-05
rope_base = 500000.0


def rope_tables(length, head_dim):
    positions = jnp.arange(length).astype(jnp.float32)
    freq_index = jnp.arange(head_dim // 2).astype(jnp.float32)
    inverse = 1.0 / rope_base ** (2.0 * freq_index / head_dim)
    angles = positions[:, None] * inverse[None, :]
    cosine = jnp.concatenate([jnp.cos(angles), jnp.cos(angles)], axis=1)
    sine = jnp.concatenate([jnp.sin(angles), jnp.sin(angles)], axis=1)
    return (cosine, sine)


MESH = pl.DeviceIdType.MESH
VMEM_BYTES = 52 * 1024 * 1024


def remote(src, dst, send_sem, recv_sem, **where):
    return pltpu.make_async_remote_copy(
        src_ref=src, dst_ref=dst, send_sem=send_sem, recv_sem=recv_sem,
        device_id=where, device_id_type=MESH,
    )


def dot_nt(left, right):
    return lax.dot_general(
        left, right, (((1,), (1,)), ((), ())), preferred_element_type=jnp.float32
    )


def dot_tn(left, right):
    return lax.dot_general(
        left, right, (((0,), (0,)), ((), ())), preferred_element_type=jnp.float32
    )


FWD_CHUNKS = 2
BWD_CHUNKS = 4


def section_kernel(
    count, stages,
    hid, gain, kw, vw, query, cotan, factor, live, cosine, sine,
    low, kg_out, vg_out,
    normed, cols, total, psend, precv, woth, inv, key_raw, val_raw,
    comb, cpart, pown, poth, ngs, ngr, cot, cother,
    zs, zr, ws, wr, fs, fr, ps, pr, ls,
    sa, ra, sb, rb, sc, rc, sn, rn, so, ro,
):
    p = lax.axis_index("pipe")
    z = lax.axis_index("dp")
    y = lax.axis_index("tensor")
    other = 1 - y
    toks, width = hid.shape
    rows = width // count
    half_rows = rows // 2
    kcols = kw.shape[1]
    chunk = toks // BWD_CHUNKS
    half = toks // 2
    fchunk = half // FWD_CHUNKS
    has_lower = p > 0
    has_upper = p < stages - 1

    barrier = pltpu.get_barrier_semaphore()
    for d in range(1, count):
        pl.semaphore_signal(
            barrier, inc=1, device_id={"dp": lax.rem(z + d, count)}, device_id_type=MESH
        )
    pl.semaphore_signal(barrier, inc=1, device_id={"tensor": other}, device_id_type=MESH)

    @pl.when(has_lower)
    def _():
        pl.semaphore_signal(barrier, inc=1, device_id={"pipe": p - 1}, device_id_type=MESH)

    @pl.when(has_upper)
    def _():
        pl.semaphore_signal(barrier, inc=1, device_id={"pipe": p + 1}, device_id_type=MESH)

    peers = count + has_lower.astype(jnp.int32) + has_upper.astype(jnp.int32)
    pl.semaphore_wait(barrier, peers)

    def norm_half(which):
        def step(i, carry):
            at = pl.ds(pl.multiple_of(which * half + i * 16, 16), 16)
            h = hid[at, :].astype(jnp.float32)
            scale_row = lax.rsqrt(jnp.mean(h * h, axis=-1, keepdims=True) + norm_eps)
            normed[at, :] = (h * scale_row * gain[...]).astype(jnp.bfloat16)
            inv[at, :] = jnp.broadcast_to(scale_row, (16, 128))
            return carry

        lax.fori_loop(0, half // 16, step, 0)

    def rows_of(which, c):
        return pl.ds(pl.multiple_of(which * half + c * fchunk, 16), fchunk)

    norm_half(y)
    sent = []
    for c in range(FWD_CHUNKS):
        for d in range(1, count):
            to = lax.rem(z + d, count)
            copy = remote(
                normed.at[rows_of(y, c), pl.ds(pl.multiple_of(to * rows, 128), rows)],
                cols.at[z, rows_of(y, c), :],
                zs.at[c, d - 1], zr.at[c, d - 1], dp=to,
            )
            copy.start()
            sent.append(copy)
    give = pl.ds(pl.multiple_of(other * half_rows, 16), half_rows)
    wcopies = [
        remote(kw.at[give, :], woth.at[0], ws.at[0], wr.at[0], tensor=other),
        remote(vw.at[give, :], woth.at[1], ws.at[1], wr.at[1], tensor=other),
    ]
    for copy in wcopies:
        copy.start()
    norm_half(other)
    own = pltpu.make_async_copy(
        normed.at[:, pl.ds(pl.multiple_of(z * rows, 128), rows)], cols.at[z], ls.at[0]
    )
    own.start()
    own.wait()

    step_k = min(rows, 512)

    def project(src, c):
        def step(k, acc):
            at = pl.ds(pl.multiple_of(k * step_k, 128), step_k)
            a = jnp.concatenate(
                [cols[src, pl.ds(c * fchunk, fchunk), at], cols[src, pl.ds(half + c * fchunk, fchunk), at]],
                axis=0,
            )
            return (
                acc[0] + jnp.dot(a, kw[at, :], preferred_element_type=jnp.float32),
                acc[1] + jnp.dot(a, vw[at, :], preferred_element_type=jnp.float32),
            )

        zero = jnp.zeros((2 * fchunk, kcols), jnp.float32)
        return lax.fori_loop(0, rows // step_k, step, (zero, zero))

    for c in range(FWD_CHUNKS):
        ka, va = project(z, c)
        total[c, :, :kcols] = ka
        total[c, :, kcols:] = va

    for c in range(FWD_CHUNKS):
        for d in range(1, count):
            src = lax.rem(z - d + count, count)
            place = cols.at[src, rows_of(y, c), :]
            remote(place, place, zs.at[c, d - 1], zr.at[c, d - 1], dp=src).wait_recv()
            copy = remote(place, place, fs.at[c, d - 1], fr.at[c, d - 1], tensor=other)
            copy.start()
            sent.append(copy)
        for d in range(1, count):
            src = lax.rem(z - d + count, count)
            place = cols.at[src, rows_of(other, c), :]
            remote(place, place, fs.at[c, d - 1], fr.at[c, d - 1], tensor=other).wait_recv()
            ka, va = project(src, c)
            psend[d - 1, c, :, :kcols] = ka.astype(jnp.bfloat16)
            psend[d - 1, c, :, kcols:] = va.astype(jnp.bfloat16)
            copy = remote(
                psend.at[d - 1, c], precv.at[d - 1, c], ps.at[c, d - 1], pr.at[c, d - 1], dp=src
            )
            copy.start()
            sent.append(copy)
    for c in range(FWD_CHUNKS):
        acc = total[c]
        for d in range(1, count):
            remote(
                psend.at[d - 1, c], precv.at[d - 1, c], ps.at[c, d - 1], pr.at[c, d - 1],
                dp=lax.rem(z + d, count),
            ).wait_recv()
            acc = acc + precv[d - 1, c].astype(jnp.float32)
        for which in range(2):
            at = pl.ds(which * half + c * fchunk, fchunk)
            part = acc[which * fchunk : (which + 1) * fchunk]
            key_raw[at, :] = part[:, :kcols]
            val_raw[at, :] = part[:, kcols:]

    lane = lax.broadcasted_iota(jnp.int32, (toks, HD), 1)
    sign = jnp.where(lane < HD // 2, -1.0, 1.0)
    key_pos = lax.broadcasted_iota(jnp.int32, (toks, toks), 0)
    query_pos = lax.broadcasted_iota(jnp.int32, (toks, toks), 1)
    allowed = (key_pos <= query_pos) & (live[...][:, :1] > 0.0)
    bias = jnp.where(allowed, 0.0, -1e30)
    scale = 1.0 / math.sqrt(HD)
    group = query.shape[1] // kcols
    weigh = factor[...][:, :1]
    cen = jnp.zeros((toks, 1), jnp.float32)
    for k in range(kcols // HD):
        head = pl.ds(k * HD, HD)
        raw = key_raw[:, head]
        key = (raw * cosine[...] + pltpu.roll(raw, HD // 2, 1) * sign * sine[...]).astype(jnp.bfloat16)
        value = val_raw[:, head].astype(jnp.bfloat16)
        vgrad = jnp.zeros((toks, HD), jnp.float32)
        rgrad = jnp.zeros((toks, HD), jnp.float32)
        for g in range(group):
            at = pl.ds((k * group + g) * HD, HD)
            q = query[:, at]
            co = (cotan[:, at].astype(jnp.float32) * weigh).astype(jnp.bfloat16)
            scores = dot_nt(key, q) * scale + bias
            expd = jnp.exp(scores - jnp.max(scores, axis=0, keepdims=True))
            probs = expd * (1.0 / jnp.sum(expd, axis=0, keepdims=True))
            pgrad = dot_nt(value, co)
            centre = jnp.sum(probs * pgrad, axis=0, keepdims=True)
            sgrad = (probs * (pgrad - centre) * scale).astype(jnp.bfloat16)
            vgrad = vgrad + jnp.dot(probs.astype(jnp.bfloat16), co, preferred_element_type=jnp.float32)
            rgrad = rgrad + jnp.dot(sgrad, q, preferred_element_type=jnp.float32)
        kgrad = rgrad * cosine[...] - pltpu.roll(rgrad * sine[...], HD // 2, 1) * sign
        klow, vlow = kgrad.astype(jnp.bfloat16), vgrad.astype(jnp.bfloat16)
        comb[:, head] = klow
        comb[:, pl.ds(kcols + k * HD, HD)] = vlow
        cen = cen + jnp.sum(
            klow.astype(jnp.float32) * raw + vlow.astype(jnp.float32) * val_raw[:, head],
            axis=1, keepdims=True,
        )
    cpart[...] = jnp.broadcast_to(cen, (toks, 128))

    for d in range(1, count):
        copy = remote(comb, pown.at[z], sa.at[d - 1], ra.at[d - 1], dp=lax.rem(z + d, count))
        copy.start()
        sent.append(copy)
    copy = remote(comb, poth.at[z], sb.at[0], rb.at[0], tensor=other)
    copy.start()
    sent.append(copy)
    ccopy = remote(cpart, cother, sc.at[0], rc.at[0], tensor=other)
    ccopy.start()
    pown[z] = comb[...]
    for d in range(1, count):
        src = lax.rem(z - d + count, count)
        remote(comb, pown.at[src], sa.at[d - 1], ra.at[d - 1], dp=src).wait_recv()
        copy = remote(pown.at[src], poth.at[src], sb.at[d], rb.at[d], tensor=other)
        copy.start()
        sent.append(copy)

    tile = min(half_rows, 256)

    def normed_grad(src, out, slot):
        def step(n, carry):
            mine = pl.ds(pl.multiple_of(y * half_rows + n * tile, 16), tile)
            at = pl.ds(pl.multiple_of(n * tile, 128), tile)
            a = dot_nt(pown[src, :, :kcols], kw[mine, :]) + dot_nt(pown[src, :, kcols:], vw[mine, :])
            b = dot_nt(poth[src, :, :kcols], woth[0, at, :]) + dot_nt(poth[src, :, kcols:], woth[1, at, :])
            both = a.astype(jnp.bfloat16).astype(jnp.float32) + b.astype(jnp.bfloat16).astype(jnp.float32)
            out[slot, :, at] = both.astype(jnp.bfloat16)
            return carry

        lax.fori_loop(0, half_rows // tile, step, 0)

    def wait_other(d):
        src = lax.rem(z - d + count, count)
        remote(pown.at[src], poth.at[src], sb.at[d], rb.at[d], tensor=other).wait_recv()

    for copy in wcopies:
        copy.wait()
    wait_other(0)
    normed_grad(z, ngr, z)
    for d in range(1, count):
        wait_other(d)
        normed_grad(lax.rem(z - d + count, count), ngs, d - 1)
    for c in range(BWD_CHUNKS):
        at = pl.ds(c * chunk, chunk)
        for d in range(1, count):
            copy = remote(
                ngs.at[d - 1, at, :], ngr.at[z, at, :], sn.at[c, d - 1], rn.at[c, d - 1],
                dp=lax.rem(z - d + count, count),
            )
            copy.start()
            sent.append(copy)
    ccopy.wait()

    wtile = min(rows, 256)
    wsteps = rows // wtile

    def weight_grad(n, carry):
        at = pl.ds(pl.multiple_of(n * wtile, 128), wtile)
        acc = jnp.zeros((wtile, 2 * kcols), jnp.float32)
        for r in range(count):
            term = dot_tn(cols[r, :, at], pown[r])
            acc = acc + term.astype(jnp.bfloat16).astype(jnp.float32)
        low_acc = acc.astype(jnp.bfloat16)
        kg_out[at, :] = low_acc[:, :kcols]
        vg_out[at, :] = low_acc[:, kcols:]
        return carry

    def out_place(c, w, which):
        feat = pl.ds(pl.multiple_of(w * rows + which * half_rows, 128), half_rows)
        return low.at[pl.ds(c * chunk, chunk), feat]

    def out_copy(c, w, to):
        src = cot.at[w, pl.ds(c * chunk, chunk), :]
        return remote(src, out_place(c, w, y), so.at[c, w, 0], ro.at[c, w, 0], pipe=to)

    def cross_copy(c, w, which):
        place = out_place(c, w, which)
        return remote(place, place, so.at[c, w, 1], ro.at[c, w, 1], tensor=other)

    def pass_on(c):
        @pl.when(has_upper)
        def _():
            for w in range(count):
                out_copy(c, w, p + 1).wait_recv()
                cross_copy(c, w, y).start()

    for c in range(BWD_CHUNKS):
        lax.fori_loop(wsteps * c // BWD_CHUNKS, wsteps * (c + 1) // BWD_CHUNKS, weight_grad, 0)
        for d in range(1, count):
            to = lax.rem(z + d, count)
            remote(
                ngs.at[d - 1, pl.ds(c * chunk, chunk), :], ngr.at[to, pl.ds(c * chunk, chunk), :],
                sn.at[c, d - 1], rn.at[c, d - 1], dp=to,
            ).wait_recv()

        def tail(i, carry):
            at = pl.ds(pl.multiple_of(c * chunk + i * 16, 16), 16)
            inv_rms = inv[at, :][:, :1]
            centre = (cpart[at, :] + cother[at, :])[:, :1] * (1.0 / width)
            for w in range(count):
                feat = pl.ds(pl.multiple_of(w * rows + y * half_rows, 128), half_rows)
                nhat = hid[at, feat].astype(jnp.float32) * inv_rms
                grad_in = ngr[w, at, :].astype(jnp.float32) * gain[:, feat]
                cot[w, at, :] = ((grad_in - nhat * centre) * inv_rms).astype(jnp.bfloat16)
            return carry

        lax.fori_loop(0, chunk // 16, tail, 0)

        @pl.when(has_lower)
        def _():
            for w in range(count):
                out_copy(c, w, p - 1).start()

        if c > 0:
            pass_on(c - 1)

    pass_on(BWD_CHUNKS - 1)

    for copy in sent:
        copy.wait_send()

    @pl.when(has_lower)
    def _():
        for c in range(BWD_CHUNKS):
            for w in range(count):
                out_copy(c, w, p - 1).wait_send()

    @pl.when(has_upper)
    def _():
        for c in range(BWD_CHUNKS):
            for w in range(count):
                cross_copy(c, w, y).wait_send()
                cross_copy(c, w, other).wait_recv()


def section_call(arrays, count, stages):
    hidden, _, kw = arrays[:3]
    toks, width = hidden.shape
    rows = width // count
    kcols = kw.shape[1]
    low, wide = jnp.bfloat16, jnp.float32
    vmem = pl.BlockSpec(memory_space=pltpu.VMEM)
    hbm = pl.BlockSpec(memory_space=pl.ANY)
    dma = pltpu.SemaphoreType.DMA
    m = toks // FWD_CHUNKS
    fpair = (FWD_CHUNKS, count - 1)
    bpair = (BWD_CHUNKS, count - 1)
    trio = (BWD_CHUNKS, count, 2)
    others = count - 1
    return pl.pallas_call(
        functools.partial(section_kernel, count, stages),
        out_shape=(
            jax.ShapeDtypeStruct((toks, width), low),
            jax.ShapeDtypeStruct((rows, kcols), low),
            jax.ShapeDtypeStruct((rows, kcols), low),
        ),
        in_specs=[vmem] * 10,
        out_specs=(hbm, vmem, vmem),
        scratch_shapes=[
            pltpu.VMEM((toks, width), low),
            pltpu.VMEM((count, toks, rows), low),
            pltpu.VMEM((FWD_CHUNKS, m, 2 * kcols), wide),
            pltpu.VMEM((others, FWD_CHUNKS, m, 2 * kcols), low),
            pltpu.VMEM((others, FWD_CHUNKS, m, 2 * kcols), low),
            pltpu.VMEM((2, rows // 2, kcols), low),
            pltpu.VMEM((toks, 128), wide),
            pltpu.VMEM((toks, kcols), wide),
            pltpu.VMEM((toks, kcols), wide),
            pltpu.VMEM((toks, 2 * kcols), low),
            pltpu.VMEM((toks, 128), wide),
            pltpu.VMEM((count, toks, 2 * kcols), low),
            pltpu.VMEM((count, toks, 2 * kcols), low),
            pltpu.VMEM((others, toks, rows // 2), low),
            pltpu.VMEM((count, toks, rows // 2), low),
            pltpu.VMEM((count, toks, rows // 2), low),
            pltpu.VMEM((toks, 128), wide),
            dma(fpair), dma(fpair), dma((2,)), dma((2,)), dma(fpair), dma(fpair), dma(fpair), dma(fpair),
            dma((1,)),
            dma((others,)), dma((others,)), dma((count,)), dma((count,)), dma((1,)), dma((1,)),
            dma(bpair), dma(bpair), dma(trio), dma(trio),
        ],
        compiler_params=pltpu.CompilerParams(
            collective_id=0, has_side_effects=True, vmem_limit_bytes=VMEM_BYTES
        ),
        name="section",
    )(*arrays)


def on_device(
    hidden_states,
    norm_gain,
    key_weight,
    value_weight,
    queries,
    context_cotangent,
    lengths,
    policy_logp,
    reference_logp,
):
    count = lax.axis_size("dp")
    stages = lax.axis_size("pipe")
    hidden = hidden_states[0]
    toks = hidden.shape[0]
    assert lengths.shape[1] == 1 and lax.axis_size("tensor") == 2
    cosine, sine = rope_tables(toks, HD)
    seq_weight = 2.0 * jax.nn.sigmoid(npo_beta * (policy_logp[0] - reference_logp[0])) / count
    live = jnp.arange(toks)[:, None] < lengths[0][None, :]
    factor = jnp.where(live, seq_weight[None, :], 0.0)
    low, kg, vg = section_call(
        (
            hidden,
            norm_gain.astype(jnp.float32),
            key_weight[0],
            value_weight[0],
            queries[0],
            context_cotangent[0],
            jnp.broadcast_to(factor, (toks, 128)),
            jnp.broadcast_to(live.astype(jnp.float32), (toks, 128)),
            cosine,
            sine,
        ),
        count,
        stages,
    )
    low = jnp.where(lax.axis_index("pipe") < stages - 1, low, jnp.zeros_like(low))
    return (kg[None], vg[None], low[None])


def solution(mesh):
    in_specs = (
        P("pipe", "dp", None),
        P("pipe", None),
        P("pipe", "dp", "tensor"),
        P("pipe", "dp", "tensor"),
        P("pipe", "dp", "tensor"),
        P("pipe", "dp", "tensor"),
        P("pipe", "dp"),
        P("pipe", "dp"),
        P("pipe", "dp"),
    )
    out_specs = (P("pipe", "dp", "tensor"), P("pipe", "dp", "tensor"), P("pipe", "dp", None))
    return jax.shard_map(
        on_device, mesh=mesh, in_specs=in_specs, out_specs=out_specs, check_vma=False
    )
```

time: 226 us -> 209 us (0.925)
  the two profiles are of different devices: /device:TPU:0 before, /device:TPU:20 now
where the time goes in v2:
time: 209 us
  Pallas kernels  198 us (95%)
  other arithmetic  6.05 us (3%)
  between operations  2.73 us (1%)
  local copies, waits for them, and re-layouts  2.12 us (1%)
    pallas_call x1, Pallas kernels, section_call(): pl.pallas_call(functools.partial(section_kernel, count, stages), out_shap...  198 us
    broadcast_in_dim x1, other arithmetic, on_device(): return (kg[None], vg[None], low[None])  4.57 us

profile of v2, /device:TPU:20, one launch (start us, length us, event | category | flops | bytes accessed | tf_op | source)
XLA Modules:
  0.0 208.7 jit_solution(16285168563517488239)
XLA Ops:
  2.7 0.8 convert_element_type.37.gain
  3.5 0.1 broadcast_in_dim.44.live
  3.6 0.1 broadcast_in_dim.43.factor
  3.7 0.5 multiply_sine_fusion
  4.2 0.1 pad_maximum_fusion
  4.4 197.8 %section.1 = (bf16[256,8192]{1,0:T(8,128)(2,1)}, bf16[2048,256]{1,0:T(8,128)(2,1)S(1)}, bf16[2048,256]{1,0:T(8,128)(2,1)}) custom-call(bf16[256,8192]{1,0:T(8,128)(2,1)} %bitcast.14, f32[1,8192]{1,0:T(1,128)S(1)} %convert_element_type.37.gain, bf16[2048,256]{1,0:T(8,128)(2,1)} %bitcast.15, bf16[2048,256]{1,0:T(8,128)(2,1)} %bitcast.16, ...), custom_call_target="tpu_custom_call" | custom-call | tf_op jit(solution)/shard_map/section/pallas_call | solution.py:381
  202.2 0.0 copy-start
  202.2 4.6 %select_bitcast_fusion = bf16[1,256,8192]{2,1,0:T(8,128)(2,1)} fusion(bf16[256,8192]{1,0:T(8,128)(2,1)} %get-tuple-element.8, pred[]{:T(512)S(6)} %lt.24), kind=kLoop, calls=%fused_computation | loop fusion | flops 2097152 | bytes 8388609 | tf_op jit(solution)/shard_map/broadcast_in_dim | solution.py:457
  206.8 1.0 copy.17
  207.7 0.0 copy-done
  207.7 1.0 copy.18
  (4 shorter events, 0.0 us)
Async XLA Ops:
  202.2 5.6 %copy-start = (bf16[2048,256]{1,0:T(8,128)(2,1)S(1)}, bf16[2048,256]{1,0:T(8,128)(2,1)}, u32[]{:S(2)}) copy-start(bf16[2048,256]{1,0:T(8,128)(2,1)} %get-tuple-element.7) | copy-start | bytes 3145732

commit v3 on v2

--- a/solution.py
+++ b/solution.py
@@ -49,15 +49,15 @@
     )
 
 
-FWD_CHUNKS = 2
-BWD_CHUNKS = 4
+FWD_CHUNKS = 4
+BWD_CHUNKS = 8
 
 
 def section_kernel(
     count, stages,
     hid, gain, kw, vw, query, cotan, factor, live, cosine, sine,
     low, kg_out, vg_out,
-    normed, cols, total, psend, precv, woth, inv, key_raw, val_raw,
+    wcat, normed, cols, total, psend, precv, woth, inv, raws,
     comb, cpart, pown, poth, ngs, ngr, cot, cother,
     zs, zr, ws, wr, fs, fr, ps, pr, ls,
     sa, ra, sb, rb, sc, rc, sn, rn, so, ro,
@@ -70,6 +70,7 @@
     rows = width // count
     half_rows = rows // 2
     kcols = kw.shape[1]
+    heads = kcols // HD
     chunk = toks // BWD_CHUNKS
     half = toks // 2
     fchunk = half // FWD_CHUNKS
@@ -91,6 +92,10 @@
     def _():
         pl.semaphore_signal(barrier, inc=1, device_id={"pipe": p + 1}, device_id_type=MESH)
 
+    for k in range(heads):
+        head = pl.ds(k * HD, HD)
+        wcat[:, pl.ds(2 * k * HD, HD)] = kw[:, head]
+        wcat[:, pl.ds((2 * k + 1) * HD, HD)] = vw[:, head]
     peers = count + has_lower.astype(jnp.int32) + has_upper.astype(jnp.int32)
     pl.semaphore_wait(barrier, peers)
 
@@ -110,23 +115,19 @@
 
     norm_half(y)
     sent = []
-    for c in range(FWD_CHUNKS):
-        for d in range(1, count):
-            to = lax.rem(z + d, count)
-            copy = remote(
-                normed.at[rows_of(y, c), pl.ds(pl.multiple_of(to * rows, 128), rows)],
-                cols.at[z, rows_of(y, c), :],
-                zs.at[c, d - 1], zr.at[c, d - 1], dp=to,
-            )
-            copy.start()
-            sent.append(copy)
+
+    def column_copy(c, d):
+        to = lax.rem(z + d, count)
+        return remote(
+            normed.at[rows_of(y, c), pl.ds(pl.multiple_of(to * rows, 128), rows)],
+            cols.at[z, rows_of(y, c), :],
+            zs.at[c, d - 1], zr.at[c, d - 1], dp=to,
+        )
+
+    for d in range(1, count):
+        column_copy(0, d).start()
     give = pl.ds(pl.multiple_of(other * half_rows, 16), half_rows)
-    wcopies = [
-        remote(kw.at[give, :], woth.at[0], ws.at[0], wr.at[0], tensor=other),
-        remote(vw.at[give, :], woth.at[1], ws.at[1], wr.at[1], tensor=other),
-    ]
-    for copy in wcopies:
-        copy.start()
+    wcopy = remote(wcat.at[give, :], woth, ws.at[0], wr.at[0], tensor=other)
     norm_half(other)
     own = pltpu.make_async_copy(
         normed.at[:, pl.ds(pl.multiple_of(z * rows, 128), rows)], cols.at[z], ls.at[0]
@@ -136,25 +137,25 @@
 
     step_k = min(rows, 512)
 
-    def project(src, c):
+    def project(sources, c):
         def step(k, acc):
             at = pl.ds(pl.multiple_of(k * step_k, 128), step_k)
-            a = jnp.concatenate(
-                [cols[src, pl.ds(c * fchunk, fchunk), at], cols[src, pl.ds(half + c * fchunk, fchunk), at]],
-                axis=0,
-            )
-            return (
-                acc[0] + jnp.dot(a, kw[at, :], preferred_element_type=jnp.float32),
-                acc[1] + jnp.dot(a, vw[at, :], preferred_element_type=jnp.float32),
-            )
-
-        zero = jnp.zeros((2 * fchunk, kcols), jnp.float32)
-        return lax.fori_loop(0, rows // step_k, step, (zero, zero))
+            parts = []
+            for src in sources:
+                parts.append(cols[src, pl.ds(c * fchunk, fchunk), at])
+                parts.append(cols[src, pl.ds(half + c * fchunk, fchunk), at])
+            a = jnp.concatenate(parts, axis=0)
+            return acc + jnp.dot(a, wcat[at, :], preferred_element_type=jnp.float32)
+
+        zero = jnp.zeros((len(sources) * 2 * fchunk, 2 * kcols), jnp.float32)
+        return lax.fori_loop(0, rows // step_k, step, zero)
 
     for c in range(FWD_CHUNKS):
-        ka, va = project(z, c)
-        total[c, :, :kcols] = ka
-        total[c, :, kcols:] = va
+        if c == 1:
+            for d in range(1, count):
+                column_copy(0, d).wait_send()
+                column_copy(1, d).start()
+        total[c] = project([z], c)
 
     for c in range(FWD_CHUNKS):
         for d in range(1, count):
@@ -164,18 +165,28 @@
             copy = remote(place, place, fs.at[c, d - 1], fr.at[c, d - 1], tensor=other)
             copy.start()
             sent.append(copy)
-        for d in range(1, count):
-            src = lax.rem(z - d + count, count)
-            place = cols.at[src, rows_of(other, c), :]
-            remote(place, place, fs.at[c, d - 1], fr.at[c, d - 1], tensor=other).wait_recv()
-            ka, va = project(src, c)
-            psend[d - 1, c, :, :kcols] = ka.astype(jnp.bfloat16)
-            psend[d - 1, c, :, kcols:] = va.astype(jnp.bfloat16)
-            copy = remote(
-                psend.at[d - 1, c], precv.at[d - 1, c], ps.at[c, d - 1], pr.at[c, d - 1], dp=src
-            )
-            copy.start()
-            sent.append(copy)
+        if c == FWD_CHUNKS - 1:
+            wcopy.start()
+        else:
+            for d in range(1, count):
+                column_copy(c + 1, d).wait_send()
+                if c < FWD_CHUNKS - 2:
+                    column_copy(c + 2, d).start()
+        for first in range(1, count, 3):
+            members = range(first, min(first + 3, count))
+            sources = [lax.rem(z - d + count, count) for d in members]
+            for d, src in zip(members, sources):
+                place = cols.at[src, rows_of(other, c), :]
+                remote(place, place, fs.at[c, d - 1], fr.at[c, d - 1], tensor=other).wait_recv()
+            part = project(sources, c).astype(jnp.bfloat16)
+            for i, d in enumerate(members):
+                psend[d - 1, c] = part[i * 2 * fchunk : (i + 1) * 2 * fchunk]
+                copy = remote(
+                    psend.at[d - 1, c], precv.at[d - 1, c], ps.at[c, d - 1], pr.at[c, d - 1],
+                    dp=sources[i],
+                )
+                copy.start()
+                sent.append(copy)
     for c in range(FWD_CHUNKS):
         acc = total[c]
         for d in range(1, count):
@@ -185,10 +196,9 @@
             ).wait_recv()
             acc = acc + precv[d - 1, c].astype(jnp.float32)
         for which in range(2):
-            at = pl.ds(which * half + c * fchunk, fchunk)
-            part = acc[which * fchunk : (which + 1) * fchunk]
-            key_raw[at, :] = part[:, :kcols]
-            val_raw[at, :] = part[:, kcols:]
+            raws[pl.ds(which * half + c * fchunk, fchunk), :] = acc[
+                which * fchunk : (which + 1) * fchunk
+            ]
 
     lane = lax.broadcasted_iota(jnp.int32, (toks, HD), 1)
     sign = jnp.where(lane < HD // 2, -1.0, 1.0)
@@ -200,11 +210,21 @@
     group = query.shape[1] // kcols
     weigh = factor[...][:, :1]
     cen = jnp.zeros((toks, 1), jnp.float32)
-    for k in range(kcols // HD):
-        head = pl.ds(k * HD, HD)
-        raw = key_raw[:, head]
+
+    def pair(k):
+        return pl.ds(2 * k * HD, 2 * HD)
+
+    def piece_copy(d, k):
+        return remote(
+            comb.at[:, pair(k)], pown.at[z, :, pair(k)], sa.at[d - 1, k], ra.at[d - 1, k],
+            dp=lax.rem(z + d, count),
+        )
+
+    for k in range(heads):
+        raw = raws[:, pl.ds(2 * k * HD, HD)]
+        val = raws[:, pl.ds((2 * k + 1) * HD, HD)]
         key = (raw * cosine[...] + pltpu.roll(raw, HD // 2, 1) * sign * sine[...]).astype(jnp.bfloat16)
-        value = val_raw[:, head].astype(jnp.bfloat16)
+        value = val.astype(jnp.bfloat16)
         vgrad = jnp.zeros((toks, HD), jnp.float32)
         rgrad = jnp.zeros((toks, HD), jnp.float32)
         for g in range(group):
@@ -221,30 +241,36 @@
             rgrad = rgrad + jnp.dot(sgrad, q, preferred_element_type=jnp.float32)
         kgrad = rgrad * cosine[...] - pltpu.roll(rgrad * sine[...], HD // 2, 1) * sign
         klow, vlow = kgrad.astype(jnp.bfloat16), vgrad.astype(jnp.bfloat16)
-        comb[:, head] = klow
-        comb[:, pl.ds(kcols + k * HD, HD)] = vlow
+        comb[:, pl.ds(2 * k * HD, HD)] = klow
+        comb[:, pl.ds((2 * k + 1) * HD, HD)] = vlow
         cen = cen + jnp.sum(
-            klow.astype(jnp.float32) * raw + vlow.astype(jnp.float32) * val_raw[:, head],
+            klow.astype(jnp.float32) * raw + vlow.astype(jnp.float32) * val,
             axis=1, keepdims=True,
         )
-    cpart[...] = jnp.broadcast_to(cen, (toks, 128))
-
-    for d in range(1, count):
-        copy = remote(comb, pown.at[z], sa.at[d - 1], ra.at[d - 1], dp=lax.rem(z + d, count))
+        for d in range(1, count):
+            copy = piece_copy(d, k)
+            copy.start()
+            sent.append(copy)
+        copy = remote(comb.at[:, pair(k)], poth.at[z, :, pair(k)], sb.at[0, k], rb.at[0, k], tensor=other)
         copy.start()
         sent.append(copy)
-    copy = remote(comb, poth.at[z], sb.at[0], rb.at[0], tensor=other)
-    copy.start()
-    sent.append(copy)
+    cpart[...] = jnp.broadcast_to(cen, (toks, 128))
     ccopy = remote(cpart, cother, sc.at[0], rc.at[0], tensor=other)
     ccopy.start()
     pown[z] = comb[...]
-    for d in range(1, count):
-        src = lax.rem(z - d + count, count)
-        remote(comb, pown.at[src], sa.at[d - 1], ra.at[d - 1], dp=src).wait_recv()
-        copy = remote(pown.at[src], poth.at[src], sb.at[d], rb.at[d], tensor=other)
-        copy.start()
-        sent.append(copy)
+
+    def cross_piece(d, k):
+        place = lax.rem(z - d + count, count)
+        return remote(
+            pown.at[place, :, pair(k)], poth.at[place, :, pair(k)], sb.at[d, k], rb.at[d, k], tensor=other
+        )
+
+    for k in range(heads):
+        for d in range(1, count):
+            piece_copy(d, k).wait_recv()
+            copy = cross_piece(d, k)
+            copy.start()
+            sent.append(copy)
 
     tile = min(half_rows, 256)
 
@@ -252,8 +278,8 @@
         def step(n, carry):
             mine = pl.ds(pl.multiple_of(y * half_rows + n * tile, 16), tile)
             at = pl.ds(pl.multiple_of(n * tile, 128), tile)
-            a = dot_nt(pown[src, :, :kcols], kw[mine, :]) + dot_nt(pown[src, :, kcols:], vw[mine, :])
-            b = dot_nt(poth[src, :, :kcols], woth[0, at, :]) + dot_nt(poth[src, :, kcols:], woth[1, at, :])
+            a = dot_nt(pown[src], wcat[mine, :])
+            b = dot_nt(poth[src], woth[at, :])
             both = a.astype(jnp.bfloat16).astype(jnp.float32) + b.astype(jnp.bfloat16).astype(jnp.float32)
             out[slot, :, at] = both.astype(jnp.bfloat16)
             return carry
@@ -261,25 +287,23 @@
         lax.fori_loop(0, half_rows // tile, step, 0)
 
     def wait_other(d):
-        src = lax.rem(z - d + count, count)
-        remote(pown.at[src], poth.at[src], sb.at[d], rb.at[d], tensor=other).wait_recv()
-
-    for copy in wcopies:
-        copy.wait()
+        for k in range(heads):
+            cross_piece(d, k).wait_recv()
+
+    def grad_copy(c, d):
+        at = pl.ds(c * chunk, chunk)
+        return remote(
+            ngs.at[d - 1, at, :], ngr.at[z, at, :], sn.at[c, d - 1], rn.at[c, d - 1],
+            dp=lax.rem(z - d + count, count),
+        )
+
+    wcopy.wait()
     wait_other(0)
     normed_grad(z, ngr, z)
     for d in range(1, count):
         wait_other(d)
         normed_grad(lax.rem(z - d + count, count), ngs, d - 1)
-    for c in range(BWD_CHUNKS):
-        at = pl.ds(c * chunk, chunk)
-        for d in range(1, count):
-            copy = remote(
-                ngs.at[d - 1, at, :], ngr.at[z, at, :], sn.at[c, d - 1], rn.at[c, d - 1],
-                dp=lax.rem(z - d + count, count),
-            )
-            copy.start()
-            sent.append(copy)
+        grad_copy(0, d).start()
     ccopy.wait()
 
     wtile = min(rows, 256)
@@ -292,8 +316,10 @@
             term = dot_tn(cols[r, :, at], pown[r])
             acc = acc + term.astype(jnp.bfloat16).astype(jnp.float32)
         low_acc = acc.astype(jnp.bfloat16)
-        kg_out[at, :] = low_acc[:, :kcols]
-        vg_out[at, :] = low_acc[:, kcols:]
+        for k in range(heads):
+            head = pl.ds(k * HD, HD)
+            kg_out[at, head] = low_acc[:, 2 * k * HD : (2 * k + 1) * HD]
+            vg_out[at, head] = low_acc[:, (2 * k + 1) * HD : (2 * k + 2) * HD]
         return carry
 
     def out_place(c, w, which):
@@ -316,13 +342,12 @@
                 cross_copy(c, w, y).start()
 
     for c in range(BWD_CHUNKS):
-        lax.fori_loop(wsteps * c // BWD_CHUNKS, wsteps * (c + 1) // BWD_CHUNKS, weight_grad, 0)
         for d in range(1, count):
-            to = lax.rem(z + d, count)
-            remote(
-                ngs.at[d - 1, pl.ds(c * chunk, chunk), :], ngr.at[to, pl.ds(c * chunk, chunk), :],
-                sn.at[c, d - 1], rn.at[c, d - 1], dp=to,
-            ).wait_recv()
+            grad_copy(c, d).wait_send()
+            if c < BWD_CHUNKS - 1:
+                grad_copy(c + 1, d).start()
+        for d in range(1, count):
+            grad_copy(c, d).wait_recv()
 
         def tail(i, carry):
             at = pl.ds(pl.multiple_of(c * chunk + i * 16, 16), 16)
@@ -342,6 +367,7 @@
             for w in range(count):
                 out_copy(c, w, p - 1).start()
 
+        lax.fori_loop(wsteps * c // BWD_CHUNKS, wsteps * (c + 1) // BWD_CHUNKS, weight_grad, 0)
         if c > 0:
             pass_on(c - 1)
 
@@ -369,6 +395,7 @@
     toks, width = hidden.shape
     rows = width // count
     kcols = kw.shape[1]
+    heads = kcols // HD
     low, wide = jnp.bfloat16, jnp.float32
     vmem = pl.BlockSpec(memory_space=pltpu.VMEM)
     hbm = pl.BlockSpec(memory_space=pl.ANY)
@@ -388,15 +415,15 @@
         in_specs=[vmem] * 10,
         out_specs=(hbm, vmem, vmem),
         scratch_shapes=[
+            pltpu.VMEM((rows, 2 * kcols), low),
             pltpu.VMEM((toks, width), low),
             pltpu.VMEM((count, toks, rows), low),
             pltpu.VMEM((FWD_CHUNKS, m, 2 * kcols), wide),
             pltpu.VMEM((others, FWD_CHUNKS, m, 2 * kcols), low),
             pltpu.VMEM((others, FWD_CHUNKS, m, 2 * kcols), low),
-            pltpu.VMEM((2, rows // 2, kcols), low),
+            pltpu.VMEM((rows // 2, 2 * kcols), low),
             pltpu.VMEM((toks, 128), wide),
-            pltpu.VMEM((toks, kcols), wide),
-            pltpu.VMEM((toks, kcols), wide),
+            pltpu.VMEM((toks, 2 * kcols), wide),
             pltpu.VMEM((toks, 2 * kcols), low),
             pltpu.VMEM((toks, 128), wide),
             pltpu.VMEM((count, toks, 2 * kcols), low),
@@ -405,9 +432,9 @@
             pltpu.VMEM((count, toks, rows // 2), low),
             pltpu.VMEM((count, toks, rows // 2), low),
             pltpu.VMEM((toks, 128), wide),
-            dma(fpair), dma(fpair), dma((2,)), dma((2,)), dma(fpair), dma(fpair), dma(fpair), dma(fpair),
+            dma(fpair), dma(fpair), dma((1,)), dma((1,)), dma(fpair), dma(fpair), dma(fpair), dma(fpair),
             dma((1,)),
-            dma((others,)), dma((others,)), dma((count,)), dma((count,)), dma((1,)), dma((1,)),
+            dma((others, heads)), dma((others, heads)), dma((count, heads)), dma((count, heads)), dma((1,)), dma((1,)),
             dma(bpair), dma(bpair), dma(trio), dma(trio),
         ],
         compiler_params=pltpu.CompilerParams(

time: 209 us -> 199 us (0.952)
  the two profiles are of different devices: /device:TPU:20 before, /device:TPU:0 now
where the time goes in v3:
time: 199 us
  Pallas kernels  188 us (94%)
  other arithmetic  6.05 us (3%)
  between operations  2.73 us (1%)
  local copies, waits for them, and re-layouts  2.12 us (1%)
    pallas_call x1, Pallas kernels, section_call(): pl.pallas_call(functools.partial(section_kernel, count, stages), out_shap...  188 us
    broadcast_in_dim x1, other arithmetic, on_device(): return (kg[None], vg[None], low[None])  4.57 us

profile of v3, /device:TPU:0, one launch (start us, length us, event | category | flops | bytes accessed | tf_op | source)
XLA Modules:
  0.0 199.0 jit_solution(14545156205288400220)
XLA Ops:
  2.7 0.8 convert_element_type.37.gain
  3.5 0.1 broadcast_in_dim.44.live
  3.6 0.1 broadcast_in_dim.43.factor
  3.7 0.5 multiply_sine_fusion
  4.2 0.1 pad_maximum_fusion
  4.4 188.1 %section.1 = (bf16[256,8192]{1,0:T(8,128)(2,1)}, bf16[2048,256]{1,0:T(8,128)(2,1)S(1)}, bf16[2048,256]{1,0:T(8,128)(2,1)}) custom-call(bf16[256,8192]{1,0:T(8,128)(2,1)} %bitcast.14, f32[1,8192]{1,0:T(1,128)S(1)} %convert_element_type.37.gain, bf16[2048,256]{1,0:T(8,128)(2,1)} %bitcast.15, bf16[2048,256]{1,0:T(8,128)(2,1)} %bitcast.16, ...), custom_call_target="tpu_custom_call" | custom-call | tf_op jit(solution)/shard_map/section/pallas_call | solution.py:408
  192.5 0.0 copy-start
  192.5 4.6 %select_bitcast_fusion = bf16[1,256,8192]{2,1,0:T(8,128)(2,1)} fusion(bf16[256,8192]{1,0:T(8,128)(2,1)} %get-tuple-element.8, pred[]{:T(512)S(6)} %lt.24), kind=kLoop, calls=%fused_computation | loop fusion | flops 2097152 | bytes 8388609 | tf_op jit(solution)/shard_map/broadcast_in_dim | solution.py:484
  197.0 1.0 copy.17
  198.0 0.0 copy-done
  198.0 1.0 copy.18
  (4 shorter events, 0.0 us)
Async XLA Ops:
  192.5 5.6 %copy-start = (bf16[2048,256]{1,0:T(8,128)(2,1)S(1)}, bf16[2048,256]{1,0:T(8,128)(2,1)}, u32[]{:S(2)}) copy-start(bf16[2048,256]{1,0:T(8,128)(2,1)} %get-tuple-element.7) | copy-start | bytes 3145732

commit v4 on v3

--- a/solution.py
+++ b/solution.py
@@ -58,9 +58,9 @@
     hid, gain, kw, vw, query, cotan, factor, live, cosine, sine,
     low, kg_out, vg_out,
     wcat, normed, cols, total, psend, precv, woth, inv, raws,
-    comb, cpart, pown, poth, ngs, ngr, cot, cother,
+    comb, cpart, pown, poth, ngs, ngr, cot, cother, stage,
     zs, zr, ws, wr, fs, fr, ps, pr, ls,
-    sa, ra, sb, rb, sc, rc, sn, rn, so, ro,
+    sa, ra, sb, rb, sc, rc, sn, rn, so, ro, sg, rg, sh,
 ):
     p = lax.axis_index("pipe")
     z = lax.axis_index("dp")
@@ -99,7 +99,7 @@
     peers = count + has_lower.astype(jnp.int32) + has_upper.astype(jnp.int32)
     pl.semaphore_wait(barrier, peers)
 
-    def norm_half(which):
+    def norm_rows(which, first, last):
         def step(i, carry):
             at = pl.ds(pl.multiple_of(which * half + i * 16, 16), 16)
             h = hid[at, :].astype(jnp.float32)
@@ -108,12 +108,12 @@
             inv[at, :] = jnp.broadcast_to(scale_row, (16, 128))
             return carry
 
-        lax.fori_loop(0, half // 16, step, 0)
+        lax.fori_loop(first // 16, last // 16, step, 0)
 
     def rows_of(which, c):
         return pl.ds(pl.multiple_of(which * half + c * fchunk, 16), fchunk)
 
-    norm_half(y)
+    norm_rows(y, 0, fchunk)
     sent = []
 
     def column_copy(c, d):
@@ -128,7 +128,8 @@
         column_copy(0, d).start()
     give = pl.ds(pl.multiple_of(other * half_rows, 16), half_rows)
     wcopy = remote(wcat.at[give, :], woth, ws.at[0], wr.at[0], tensor=other)
-    norm_half(other)
+    norm_rows(y, fchunk, half)
+    norm_rows(other, 0, half)
     own = pltpu.make_async_copy(
         normed.at[:, pl.ds(pl.multiple_of(z * rows, 128), rows)], cols.at[z], ls.at[0]
     )
@@ -304,6 +305,8 @@
         wait_other(d)
         normed_grad(lax.rem(z - d + count, count), ngs, d - 1)
         grad_copy(0, d).start()
+    for d in range(1, count):
+        grad_copy(1, d).start()
     ccopy.wait()
 
     wtile = min(rows, 256)
@@ -334,18 +337,48 @@
         place = out_place(c, w, which)
         return remote(place, place, so.at[c, w, 1], ro.at[c, w, 1], tensor=other)
 
+    first_staged = count // 2
+    staging = has_lower & (lax.rem(p, 2) == 0)
+    passes_all = has_upper & (lax.rem(p, 2) == 0)
+
+    def stage_copy(c, w):
+        at = pl.ds(c * chunk, chunk)
+        i = w - first_staged
+        return remote(
+            cot.at[w, at, :], stage.at[i, at, :], sg.at[c, i], rg.at[c, i], tensor=other
+        )
+
+    def staged_out(c, w):
+        i = w - first_staged
+        return remote(
+            stage.at[i, pl.ds(c * chunk, chunk), :], out_place(c, w, other),
+            sh.at[c, i], ro.at[c, w, 1], pipe=p - 1,
+        )
+
     def pass_on(c):
+        @pl.when(staging)
+        def _():
+            for w in range(first_staged, count):
+                stage_copy(c, w).wait_recv()
+                staged_out(c, w).start()
+
         @pl.when(has_upper)
         def _():
             for w in range(count):
                 out_copy(c, w, p + 1).wait_recv()
+                if w < first_staged:
+                    cross_copy(c, w, y).start()
+
+        @pl.when(passes_all)
+        def _():
+            for w in range(first_staged, count):
                 cross_copy(c, w, y).start()
 
     for c in range(BWD_CHUNKS):
         for d in range(1, count):
             grad_copy(c, d).wait_send()
-            if c < BWD_CHUNKS - 1:
-                grad_copy(c + 1, d).start()
+            if c < BWD_CHUNKS - 2:
+                grad_copy(c + 2, d).start()
         for d in range(1, count):
             grad_copy(c, d).wait_recv()
 
@@ -367,6 +400,11 @@
             for w in range(count):
                 out_copy(c, w, p - 1).start()
 
+        @pl.when(staging)
+        def _():
+            for w in range(first_staged, count):
+                stage_copy(c, w).start()
+
         lax.fori_loop(wsteps * c // BWD_CHUNKS, wsteps * (c + 1) // BWD_CHUNKS, weight_grad, 0)
         if c > 0:
             pass_on(c - 1)
@@ -386,8 +424,22 @@
     def _():
         for c in range(BWD_CHUNKS):
             for w in range(count):
+                if w < first_staged:
+                    cross_copy(c, w, y).wait_send()
+                cross_copy(c, w, other).wait_recv()
+
+    @pl.when(passes_all)
+    def _():
+        for c in range(BWD_CHUNKS):
+            for w in range(first_staged, count):
                 cross_copy(c, w, y).wait_send()
-                cross_copy(c, w, other).wait_recv()
+
+    @pl.when(staging)
+    def _():
+        for c in range(BWD_CHUNKS):
+            for w in range(first_staged, count):
+                stage_copy(c, w).wait_send()
+                staged_out(c, w).wait_send()
 
 
 def section_call(arrays, count, stages):
@@ -404,6 +456,7 @@
     fpair = (FWD_CHUNKS, count - 1)
     bpair = (BWD_CHUNKS, count - 1)
     trio = (BWD_CHUNKS, count, 2)
+    staged = (BWD_CHUNKS, count - count // 2)
     others = count - 1
     return pl.pallas_call(
         functools.partial(section_kernel, count, stages),
@@ -432,10 +485,11 @@
             pltpu.VMEM((count, toks, rows // 2), low),
             pltpu.VMEM((count, toks, rows // 2), low),
             pltpu.VMEM((toks, 128), wide),
+            pltpu.VMEM((count - count // 2, toks, rows // 2), low),
             dma(fpair), dma(fpair), dma((1,)), dma((1,)), dma(fpair), dma(fpair), dma(fpair), dma(fpair),
             dma((1,)),
             dma((others, heads)), dma((others, heads)), dma((count, heads)), dma((count, heads)), dma((1,)), dma((1,)),
-            dma(bpair), dma(bpair), dma(trio), dma(trio),
+            dma(bpair), dma(bpair), dma(trio), dma(trio), dma(staged), dma(staged), dma(staged),
         ],
         compiler_params=pltpu.CompilerParams(
             collective_id=0, has_side_effects=True, vmem_limit_bytes=VMEM_BYTES

time: 199 us -> 196 us (0.985)
  Pallas kernels: 188 us -> 185 us
    pallas_call x1, Pallas kernels: 188 us -> 185 us  [section_call(): pl.pallas_call(functools.partial(section_kernel, count, stages), out_shap...]
where the time goes in v4:
time: 196 us
  Pallas kernels  185 us (94%)
  other arithmetic  6.05 us (3%)
  between operations  2.73 us (1%)
  local copies, waits for them, and re-layouts  2.12 us (1%)
    pallas_call x1, Pallas kernels, section_call(): pl.pallas_call(functools.partial(section_kernel, count, stages), out_shap...  185 us
    broadcast_in_dim x1, other arithmetic, on_device(): return (kg[None], vg[None], low[None])  4.57 us

profile of v4, /device:TPU:0, one launch (start us, length us, event | category | flops | bytes accessed | tf_op | source)
XLA Modules:
  0.0 196.2 jit_solution(1787267813184704626)
XLA Ops:
  2.7 0.8 convert_element_type.37.gain
  3.5 0.1 broadcast_in_dim.44.live
  3.6 0.1 broadcast_in_dim.43.factor
  3.7 0.5 multiply_sine_fusion
  4.2 0.1 pad_maximum_fusion
  4.4 185.3 %section.1 = (bf16[256,8192]{1,0:T(8,128)(2,1)}, bf16[2048,256]{1,0:T(8,128)(2,1)S(1)}, bf16[2048,256]{1,0:T(8,128)(2,1)}) custom-call(bf16[256,8192]{1,0:T(8,128)(2,1)} %bitcast.14, f32[1,8192]{1,0:T(1,128)S(1)} %convert_element_type.37.gain, bf16[2048,256]{1,0:T(8,128)(2,1)} %bitcast.15, bf16[2048,256]{1,0:T(8,128)(2,1)} %bitcast.16, ...), custom_call_target="tpu_custom_call" | custom-call | tf_op jit(solution)/shard_map/section/pallas_call | solution.py:461
  189.7 0.0 copy-start
  189.7 4.6 %select_bitcast_fusion = bf16[1,256,8192]{2,1,0:T(8,128)(2,1)} fusion(bf16[256,8192]{1,0:T(8,128)(2,1)} %get-tuple-element.8, pred[]{:T(512)S(6)} %lt.24), kind=kLoop, calls=%fused_computation | loop fusion | flops 2097152 | bytes 8388609 | tf_op jit(solution)/shard_map/broadcast_in_dim | solution.py:538
  194.3 1.0 copy.17
  195.2 0.0 copy-done
  195.2 1.0 copy.18
  (4 shorter events, 0.0 us)
Async XLA Ops:
  189.7 5.6 %copy-start = (bf16[2048,256]{1,0:T(8,128)(2,1)S(1)}, bf16[2048,256]{1,0:T(8,128)(2,1)}, u32[]{:S(2)}) copy-start(bf16[2048,256]{1,0:T(8,128)(2,1)} %get-tuple-element.7) | copy-start | bytes 3145732

commit v5 on v4

--- a/solution.py
+++ b/solution.py
@@ -405,10 +405,11 @@
             for w in range(first_staged, count):
                 stage_copy(c, w).start()
 
+        if c > 1:
+            pass_on(c - 2)
         lax.fori_loop(wsteps * c // BWD_CHUNKS, wsteps * (c + 1) // BWD_CHUNKS, weight_grad, 0)
-        if c > 0:
-            pass_on(c - 1)
-
+
+    pass_on(BWD_CHUNKS - 2)
     pass_on(BWD_CHUNKS - 1)
 
     for copy in sent:

time: 196 us -> 199 us (1.015)
  Pallas kernels: 185 us -> 188 us
    pallas_call x1, Pallas kernels: 185 us -> 188 us  [section_call(): pl.pallas_call(functools.partial(section_kernel, count, stages), out_shap...]
where the time goes in v5:
time: 199 us
  Pallas kernels  188 us (94%)
  other arithmetic  6.05 us (3%)
  between operations  2.73 us (1%)
  local copies, waits for them, and re-layouts  2.12 us (1%)
    pallas_call x1, Pallas kernels, section_call(): pl.pallas_call(functools.partial(section_kernel, count, stages), out_shap...  188 us
    broadcast_in_dim x1, other arithmetic, on_device(): return (kg[None], vg[None], low[None])  4.57 us

profile of v5, /device:TPU:0, one launch (start us, length us, event | category | flops | bytes accessed | tf_op | source)
XLA Modules:
  0.0 198.7 jit_solution(11665447790108765952)
XLA Ops:
  2.7 0.8 convert_element_type.37.gain
  3.5 0.1 broadcast_in_dim.44.live
  3.6 0.1 broadcast_in_dim.43.factor
  3.7 0.5 multiply_sine_fusion
  4.2 0.1 pad_maximum_fusion
  4.4 187.8 %section.1 = (bf16[256,8192]{1,0:T(8,128)(2,1)}, bf16[2048,256]{1,0:T(8,128)(2,1)S(1)}, bf16[2048,256]{1,0:T(8,128)(2,1)}) custom-call(bf16[256,8192]{1,0:T(8,128)(2,1)} %bitcast.14, f32[1,8192]{1,0:T(1,128)S(1)} %convert_element_type.37.gain, bf16[2048,256]{1,0:T(8,128)(2,1)} %bitcast.15, bf16[2048,256]{1,0:T(8,128)(2,1)} %bitcast.16, ...), custom_call_target="tpu_custom_call" | custom-call | tf_op jit(solution)/shard_map/section/pallas_call | solution.py:462
  192.2 0.0 copy-start
  192.2 4.6 %select_bitcast_fusion = bf16[1,256,8192]{2,1,0:T(8,128)(2,1)} fusion(bf16[256,8192]{1,0:T(8,128)(2,1)} %get-tuple-element.8, pred[]{:T(512)S(6)} %lt.24), kind=kLoop, calls=%fused_computation | loop fusion | flops 2097152 | bytes 8388609 | tf_op jit(solution)/shard_map/broadcast_in_dim | solution.py:539
  196.8 1.0 copy.17
  197.8 0.0 copy-done
  197.8 1.0 copy.18
  (4 shorter events, 0.0 us)
Async XLA Ops:
  192.2 5.6 %copy-start = (bf16[2048,256]{1,0:T(8,128)(2,1)S(1)}, bf16[2048,256]{1,0:T(8,128)(2,1)}, u32[]{:S(2)}) copy-start(bf16[2048,256]{1,0:T(8,128)(2,1)} %get-tuple-element.7) | copy-start | bytes 3145732
